TPU v7x, 32 devices: a whole 2x2x4 slice. The times are simulated.
32 devices in a mesh: seq: 8 (over z, y), ch: 4 (over x, core).
Axes of the slice: x: 2, y: 2, z: 4, core: 2. Of those that a mesh axis runs over, the one named last changes fastest.
Arguments:
- tokens: bfloat16 [1024, 4096], P('seq', 'ch'), may hold values from -6 to 6
- norm_gain: float32 [4096], replicated, may hold values from 0.5 to 1.5
- in_proj: bfloat16 [4096, 2, 8192], P('seq', None, 'ch'), may hold values from -0.09375 to 0.09375
- conv_weight: float32 [4, 8192], P(None, 'ch'), may hold values from -3 to 3
- conv_bias: float32 [8192], P('ch'), may hold values from -2 to 2
- x_proj: bfloat16 [8192, 544], P('ch'), may hold values from -0.0625 to 0.0625
- dt_proj: bfloat16 [512, 8192], P(None, 'ch'), may hold values from -0.25 to 0.25
- dt_bias: float32 [8192], P('ch'), may hold values from -4 to 1
- a_log: float32 [8192, 16], P('ch'), as said below
- d_skip: float32 [8192], P('ch'), may hold values from -32 to 32
- out_proj: bfloat16 [8192, 4096], P('ch', 'seq'), may hold values from -0.0625 to 0.0625
Outputs:
- mixed: bfloat16 [1024, 4096], P('seq', 'ch')
Inputs may be any that keep to these rules, and one draw needn't show every extreme that they name: Every entry of a_log lies between ln(0.2 / 1024) and ln(0.2).
All inputs are finite; a program needn't handle non-finite values.
Results may differ from a plain program's by a relative error of at most 0.014.
Values may be sent and summed in bfloat16 or wider, within the bound.
A program may use at most 128 MiB of HBM per device.

v0:
```python
import jax
import jax.numpy as jnp
from jax import lax
from jax.sharding import PartitionSpec as P


def passed_along(block, axis, distance):
    devices = range(lax.axis_size(axis))
    route = [(i - distance, i) for i in devices if i - distance in devices]
    return lax.ppermute(block, axis, route)


def chain_combine(earlier, later):
    return (earlier[0] * later[0], later[0] * earlier[1] + later[1])


def on_device(
    tokens,
    norm_gain,
    in_proj,
    conv_weight,
    conv_bias,
    x_proj,
    dt_proj,
    dt_bias,
    a_log,
    d_skip,
    out_proj,
):
    token_rows = lax.all_gather(tokens, "ch", axis=1, tiled=True)
    tokens_wide = token_rows.astype(jnp.float32)
    scale_rows = lax.rsqrt(jnp.mean(tokens_wide * tokens_wide, axis=-1, keepdims=True) + 1e-06)
    normed = (tokens_wide * scale_rows * norm_gain).astype(jnp.bfloat16)
    local_tokens = normed.shape[0]
    channels = in_proj.shape[2]
    earlier_rows = passed_along(normed[-3:], "seq", 1)
    rows_all = jnp.concatenate([earlier_rows, normed], 0)
    both = jnp.einsum(
        "td,dke->tke",
        rows_all,
        lax.all_gather(in_proj, "seq", axis=0, tiled=True),
        preferred_element_type=jnp.float32,
    )
    earlier_input = both[:3, 0, :].astype(jnp.bfloat16)
    both = both[3:]
    conv_input = both[:, 0, :].astype(jnp.bfloat16)
    gate = both[:, 1, :].astype(jnp.bfloat16)
    padded = jnp.concatenate([earlier_input, conv_input], 0).astype(jnp.float32)
    convolved = conv_bias + conv_weight[0] * padded[0:local_tokens]
    for tap in range(1, 4):
        convolved = convolved + conv_weight[tap] * padded[tap : tap + local_tokens]
    activated = jax.nn.silu(convolved)
    partial_features = jnp.dot(
        activated.astype(jnp.bfloat16), x_proj, preferred_element_type=jnp.float32
    )
    features = lax.psum(partial_features, "ch")
    rank = dt_proj.shape[0]
    states = a_log.shape[1]
    step_raw = features[:, :rank].astype(jnp.bfloat16)
    b_matrix = features[:, rank : rank + states]
    c_matrix = features[:, rank + states :]
    step_size = jax.nn.softplus(
        jnp.dot(step_raw, dt_proj, preferred_element_type=jnp.float32) + dt_bias
    )
    block_width = min(128, channels)
    block_count = channels // block_width
    sub_length = min(16, local_tokens)
    sub_count = local_tokens // sub_length
    a_blocks = (-jnp.exp(a_log)).T.reshape(states, block_count, block_width).transpose(1, 0, 2)
    step_blocks = step_size.reshape(local_tokens, block_count, block_width).transpose(1, 0, 2)
    act_blocks = activated.reshape(local_tokens, block_count, block_width).transpose(1, 0, 2)
    b_sub = b_matrix.reshape(sub_count, sub_length, states, 1)
    c_sub = c_matrix.reshape(sub_count, sub_length, states, 1)

    def block_scan(block_inputs):
        step_block, act_block, a_block = block_inputs
        log_decay = (step_block[:, None, :] * a_block[None]).reshape(
            sub_count, sub_length, states, block_width
        )
        driven = (step_block * act_block).reshape(sub_count, sub_length, 1, block_width) * b_sub
        running_log = jnp.cumsum(log_decay, axis=1)
        inner = jnp.exp(running_log) * jnp.cumsum(jnp.exp(-running_log) * driven, axis=1)
        sub_decay = jnp.exp(running_log[:, -1])
        _, sub_ends = lax.associative_scan(chain_combine, (sub_decay, inner[:, -1]), axis=0)
        entering = jnp.concatenate([jnp.zeros_like(sub_ends[:1]), sub_ends[:-1]], 0)
        full_states = inner + jnp.exp(running_log) * entering[:, None]
        local_out = jnp.sum(full_states * c_sub, axis=2).reshape(local_tokens, block_width)
        return (local_out, sub_ends[-1])

    local_outs, end_states = lax.map(block_scan, (step_blocks, act_blocks, a_blocks))
    lower_ones = (
        lax.broadcasted_iota(jnp.int32, (local_tokens, local_tokens), 0)
        >= lax.broadcasted_iota(jnp.int32, (local_tokens, local_tokens), 1)
    ).astype(jnp.float32)
    cumulative = jnp.dot(lower_ones, step_size, precision=lax.Precision.HIGHEST)
    cum_blocks = cumulative.reshape(local_tokens, block_count, block_width).transpose(1, 0, 2)
    whole_decay = jnp.exp(a_blocks * cum_blocks[:, -1, None, :])

    def relay(turn, arriving):
        leaving = whole_decay * arriving + end_states
        return passed_along(leaving, "seq", 1)

    incoming = lax.fori_loop(0, lax.axis_size("seq") - 1, relay, jnp.zeros_like(end_states))

    def block_correct(block_inputs):
        cum_block, a_block, start_state = block_inputs
        carried = jnp.exp(cum_block[:, None, :] * a_block[None]) * start_state[None]
        return jnp.sum(carried * c_matrix[:, :, None], axis=1)

    corrections = lax.map(block_correct, (cum_blocks, a_blocks, incoming))
    outputs_ssm = (local_outs + corrections).transpose(1, 0, 2).reshape(local_tokens, channels)
    scanned = outputs_ssm + d_skip * activated
    gated = (scanned * jax.nn.silu(gate.astype(jnp.float32))).astype(jnp.bfloat16)
    partial_out = jnp.dot(
        gated,
        lax.all_gather(out_proj, "seq", axis=1, tiled=True),
        preferred_element_type=jnp.float32,
    )
    mixed = lax.psum_scatter(
        partial_out.astype(jnp.bfloat16), "ch", scatter_dimension=1, tiled=True
    )
    return mixed


def solution(mesh):
    placed = (
        P("seq", "ch"),
        P(),
        P("seq", None, "ch"),
        P(None, "ch"),
        P("ch"),
        P("ch", None),
        P(None, "ch"),
        P("ch"),
        P("ch", None),
        P("ch"),
        P("ch", "seq"),
    )
    return jax.shard_map(
        on_device, mesh=mesh, in_specs=placed, out_specs=P("seq", "ch"), check_vma=False
    )
```

profile of v0, /device:TPU:2, one launch (start us, length us, event | category | flops | bytes accessed | tf_op | source)
XLA Modules:
  0.0 1031.5 jit_solution(15456842504034087281)
XLA Ops:
  7.3 6.1 copy.65
  13.5 12.2 %all-gather.4.cloned.1.call-done = bf16[128,4096]{1,0:T(8,128)(2,1)} async-done(((bf16[128,1024]{1,0:T(8,128)(2,1)}), bf16[128,4096]{1,0:T(8,128)(2,1)}) %all-gather.4.cloned.1.call-update) | async-done | bytes 1048592 | tf_op jit(solution)/shard_map/all_gather | solution.py:30
  28.9 3.6 collective-permute-start.1
  34.1 632.1 %all-gather.6.cloned.1.call-done = bf16[4096,2,2048]{2,0,1:T(8,128)(2,1)} async-done(((bf16[512,2,2048]{2,0,1:T(8,128)(2,1)}), bf16[4096,2,2048]{2,0,1:T(8,128)(2,1)}) %all-gather.6.cloned.1.call-update) | async-done | bytes 33554448 | tf_op jit(solution)/shard_map/all_gather | solution.py:41
  666.2 13.2 %convolution_convert_fusion.1 = bf16[131,2,2048]{2,0,1:T(8,128)(2,1)S(1)} fusion(bf16[4096,2,2048]{2,0,1:T(8,128)(2,1)} %all-gather.6.cloned.1.call-done, bf16[128,4096]{1,0:T(8,128)(2,1)S(1)} %fusion.19, bf16[3,4096]{1,0:T(4,128)(2,1)S(1)} %collective-permute-done.1), kind=kOutput, calls=%fused_computation.48 | convolution fusion | flops 4398313472 | bytes 35700736 | tf_op jit(solution)/shard_map/td,dke->tke/dot_general | solution.py:38
  686.6 27.6 %all-reduce.9.cloned.1.call-done = f32[128,544]{0,1:T(8,128)} async-done(((f32[128,544]{0,1:T(8,128)}), f32[128,544]{0,1:T(8,128)}) %all-reduce.9.cloned.1.call-update) | async-done | bytes 278544 | tf_op jit(solution)/shard_map/psum | solution.py:56
  721.4 121.9 %while.32 = (s32[]{:T(128)}, f32[16,128,128]{2,1,0:T(8,128)}, f32[16,16,128]{2,1,0:T(8,128)S(1)}, f32[16,128,128]{2,1,0:T(8,128)}, f32[16,16,128]{2,1,0:T(8,128)...) while((s32[]{:T(128)}, f32[16,128,128]{2,1,0:T(8,128)}, ...), condition=%wide.region_6.7_spmd, body=%wide.region_2.6_spmd.sunk | while | flops 10590210 | bytes 11158153 | solution.py:90
  723.1 3.4 fusion.64
  730.8 3.4 fusion.64
  753.6 3.4 fusion.64
  768.8 3.4 fusion.64
  784.1 3.4 fusion.64
  806.9 3.4 fusion.64
  814.5 3.4 fusion.64
  822.2 3.4 fusion.64
  829.8 3.4 fusion.64
  837.4 3.4 fusion.64
  845.6 83.3 %while.33 = (s32[]{:T(128)}, f32[16,16,128]{2,1,0:T(8,128)S(1)}, f32[16,16,128]{2,1,0:T(8,128)S(1)}, f32[16,16,128]{2,1,0:T(8,128)S(1)}, s32[]{:T(128)}) while((s32[]{:T(128)}, f32[16,16,128]{2,1,0:T(8,128)S(1)}, f32[16,16,128]{2,1,0:T(8,128)S(1)}, f32[16,16,128]{2,1,0:T(8,128)S(1)}, s32[]{:T(128)}) %tuple.83), condition=%wide.region_8.9_spmd, body=%wide.region_7.8_spmd.sunk | while | flops 65538 | bytes 1048677 | solution.py:103
  845.6 3.9 collective-permute-start
  849.5 6.1 collective-permute-done
  855.6 4.4 collective-permute-start
  860.0 5.8 collective-permute-done
  865.9 4.4 collective-permute-start
  870.3 5.6 collective-permute-done
  875.9 8.9 collective-permute-start
  884.8 5.2 collective-permute-done
  890.1 15.7 %collective-permute-start = (f32[16,16,128]{2,1,0:T(8,128)S(1)}, f32[16,16,128]{2,1,0:T(8,128)S(1)}, u32[]{:S(2)}, u32[]{:S(2)}) collective-permute-start(f32[16,16,128]{2,1,0:T(8,128)S(1)} %multiply_add_fusion.2), channel_id=1, source_target_pairs={{0,4},{4,8},{8,12},{12,16},{16,20},{20,24},{24,28},{1,5},{5,9},{9,... | collective-permute-start | bytes 393224 | tf_op jit(solution)/shard_map/while/body/eval_jaxpr/ppermute | solution.py:10
  908.5 7.3 collective-permute-start
  918.4 8.0 collective-permute-start
  930.0 27.8 %while.34 = (s32[]{:T(128)}, f32[16,128,128]{2,1,0:T(8,128)}, f32[16,128,128]{2,1,0:T(8,128)S(1)}, f32[16,16,128]{2,1,0:T(8,128)}, f32[16,16,128]{2,1,0:T(8,128)S(1)}, /*index=5*/f32[128,16]{1,0:T(8,128)S(1)}, s32[]{:T(128)}) while((s32[]{:T(128)}, f32[16,128,128]{2,1,0:T(8,128)}, f32[16,128,128]{2,1,0:T(8,128)S(1)}, ...), condition=%wide.region_11.12_spmd, body=%wide.region_9.11_spmd.sunk | while | flops 1032194 | bytes 451157 | solution.py:110
  957.9 10.5 %convolution_convert_fusion = bf16[128,4096]{1,0:T(8,128)(2,1)} fusion(bf16[2048,4096]{1,0:T(8,128)(2,1)} %all-gather.8.cloned.1.call-done, f32[128,2048]{1,0:T(8,128)} %copy-done.4, bf16[131,2,2048]{2,0,1:T(8,128)(2,1)S(1)} %copy-done.3, f32[2048]{0:T(1024)S(1)} %copy-done.13, f32[16,128,128]{2,1,0:T(8,128)} %get-tuple-element.102, ...), kind=kOutput, calls=%fused_computation.46 | convolution fusion | flops 2150629376 | bytes 21504000 | tf_op jit(solution)/shard_map/dot_general | solution.py:114
  968.4 56.6 %reduce-scatter.2.cloned.1.call-done = bf16[128,1024]{1,0:T(8,128)(2,1)} async-done(((bf16[128,4096]{1,0:T(8,128)(2,1)}), bf16[128,1024]{1,0:T(8,128)(2,1)}) %reduce-scatter.2.cloned.1.call-update) | async-done | bytes 262160 | tf_op jit(solution)/shard_map/reduce_scatter | solution.py:119
  (598 shorter events, 143.3 us)
Async XLA Ops:
  6.5 675.3 %copy-start = (bf16[2048,544]{0,1:T(8,128)(2,1)S(1)}, bf16[2048,544]{0,1:T(8,128)(2,1)}, u32[]{:S(2)}) copy-start(bf16[2048,544]{0,1:T(8,128)(2,1)} %param.22) | copy-start | bytes 6684676
  6.5 19.2 %all-gather.4.cloned.1.call-start = ((), (), s32[]{:S(2)}) async-start(), calls=%async_computation.1 | async-start | bytes 1310720 | tf_op jit(solution)/shard_map/all_gather | solution.py:30
  7.3 659.0 %all-gather.6.cloned.1.call-start = ((), (), s32[]{:S(2)}) async-start(), calls=%async_computation.2 | async-start | bytes 37748736 | tf_op jit(solution)/shard_map/all_gather | solution.py:41
  13.4 13.9 %copy-start.11 = (f32[4096]{0:T(1024)S(1)}, f32[4096]{0:T(1024)}, u32[]{:S(2)}) copy-start(f32[4096]{0:T(1024)} %param.18) | copy-start | bytes 49156
  13.5 19.0 %copy-start.10 = (f32[4,2048]{1,0:T(4,128)S(1)}, f32[4,2048]{1,0:T(4,128)}, u32[]{:S(2)}) copy-start(f32[4,2048]{1,0:T(4,128)} %param.20) | copy-start | bytes 98308
  13.5 700.7 %all-reduce.9.cloned.1.call-start = ((), (), s32[]{:S(2)}) async-start(), calls=%async_computation.3 | async-start | bytes 557056 | tf_op jit(solution)/shard_map/psum | solution.py:56
  28.9 5.2 collective-permute-start.1
  679.4 1.4 copy-start.2
  679.4 0.7 copy-start.9
  680.8 1.0 copy-start.4
  681.8 2.3 copy-start.8
  683.3 274.6 %all-gather.8.cloned.1.call-start = ((), (), s32[]{:S(2)}) async-start(), calls=%async_computation.4 | async-start | bytes 18874368 | tf_op jit(solution)/shard_map/all_gather | solution.py:116
  683.9 341.1 %reduce-scatter.2.cloned.1.call-start = ((), (), s32[]{:S(2)}) async-start(), calls=%async_computation.5 | async-start | bytes 1310720 | tf_op jit(solution)/shard_map/reduce_scatter | solution.py:119
  684.2 2.4 copy-start.6
  684.9 30.8 %copy-start.12 = (f32[2048]{0:T(1024)S(1)}, f32[2048]{0:T(1024)}, u32[]{:S(2)}) copy-start(f32[2048]{0:T(1024)} %param.24) | copy-start | bytes 24580
  718.3 2.0 copy-start.5
  843.4 2.1 copy-start.7
  845.6 10.0 collective-permute-start
  855.6 10.2 collective-permute-start
  865.9 10.0 collective-permute-start
  875.9 14.1 %collective-permute-start = (f32[16,16,128]{2,1,0:T(8,128)S(1)}, f32[16,16,128]{2,1,0:T(8,128)S(1)}, u32[]{:S(2)}, u32[]{:S(2)}) collective-permute-start(f32[16,16,128]{2,1,0:T(8,128)S(1)} %multiply_add_fusion.2), channel_id=1, source_target_pairs={{0,4},{4,8},{8,12},{12,16},{16,20},{20,24},{24,28},{1,5},{5,9},{9,... | collective-permute-start | bytes 393224 | tf_op jit(solution)/shard_map/while/body/eval_jaxpr/ppermute | solution.py:10
  890.1 18.4 %collective-permute-start = (f32[16,16,128]{2,1,0:T(8,128)S(1)}, f32[16,16,128]{2,1,0:T(8,128)S(1)}, u32[]{:S(2)}, u32[]{:S(2)}) collective-permute-start(f32[16,16,128]{2,1,0:T(8,128)S(1)} %multiply_add_fusion.2), channel_id=1, source_target_pairs={{0,4},{4,8},{8,12},{12,16},{16,20},{20,24},{24,28},{1,5},{5,9},{9,... | collective-permute-start | bytes 393224 | tf_op jit(solution)/shard_map/while/body/eval_jaxpr/ppermute | solution.py:10
  908.5 9.8 collective-permute-start
  918.4 10.5 %collective-permute-start = (f32[16,16,128]{2,1,0:T(8,128)S(1)}, f32[16,16,128]{2,1,0:T(8,128)S(1)}, u32[]{:S(2)}, u32[]{:S(2)}) collective-permute-start(f32[16,16,128]{2,1,0:T(8,128)S(1)} %multiply_add_fusion.2), channel_id=1, source_target_pairs={{0,4},{4,8},{8,12},{12,16},{16,20},{20,24},{24,28},{1,5},{5,9},{9,... | collective-permute-start | bytes 393224 | tf_op jit(solution)/shard_map/while/body/eval_jaxpr/ppermute | solution.py:10
  928.9 29.0 %copy-start.3 = (bf16[131,2,2048]{2,0,1:T(8,128)(2,1)S(1)}, bf16[131,2,2048]{2,0,1:T(8,128)(2,1)}, u32[]{:S(2)}) copy-start(bf16[131,2,2048]{2,0,1:T(8,128)(2,1)} %copy-done.2) | copy-start | bytes 3219460
  930.0 27.9 %copy-start.13 = (f32[2048]{0:T(1024)S(1)}, f32[2048]{0:T(1024)}, u32[]{:S(2)}) copy-start(f32[2048]{0:T(1024)} %param.26) | copy-start | bytes 24580
  957.9 67.1 %copy-start.1 = (bf16[2048,544]{0,1:T(8,128)(2,1)S(1)}, bf16[2048,544]{0,1:T(8,128)(2,1)}, u32[]{:S(2)}) copy-start(bf16[2048,544]{0,1:T(8,128)(2,1)} %param.22) | copy-start | bytes 6684676
Sparse Core Ops, SparseCore 0:
  8.9 16.7 all-gather.3
  27.3 638.8 all-gather.5
  683.4 30.6 all-reduce.8
  716.1 240.0 all-gather.7
  968.5 56.4 reduce-scatter.1
where the time goes:
time: 1040 us; the launch traced here: 1030 us
  waiting for transfers between devices  762 us (73%)
  other arithmetic  92.4 us (9%)
  local copies, waits for them, and re-layouts  73.9 us (7%)
  starting transfers between devices  56.5 us (5%)
  matrix products  29.7 us (3%)
  between operations  13.4 us (1%)
    all_gather x1, waiting for transfers between devices, on_device(): lax.all_gather(in_proj, 'seq', axis=0, tiled=True)  632 us
    reduce_scatter x1, waiting for transfers between devices, on_device(): lax.psum_scatter(partial_out.astype(jnp.bfloat16), 'ch', scatter_dimensio...  56.6 us
    ppermute x8, starting transfers between devices, passed_along(): return lax.ppermute(block, axis, route)  56.2 us
    another operation x16, other arithmetic, block_scan(): jnp.cumsum(jnp.exp(-running_log) * driven, axis=1)  54.1 us
    ppermute x8, waiting for transfers between devices, passed_along(): return lax.ppermute(block, axis, route)  32 us
    psum x1, waiting for transfers between devices, on_device(): features = lax.psum(partial_features, 'ch')  27.6 us
  transfers between devices with their start and end apart: 13, of which 12 were waited for; matrix products, arithmetic and copies ran while one was open for 16% of the time, Pallas kernels for 0%

commit v1 on v0

v1 whole, which is shorter than its diff:
```python
import functools
import math

import jax
import jax.numpy as jnp
from jax import lax
from jax.experimental import pallas as pl
from jax.experimental.pallas import tpu as pltpu
from jax.sharding import PartitionSpec as P

TAPS = 4
CHUNK = 128


def scan_kernel(
    conv_input,
    gate,
    step_raw,
    b_rows,
    c_rows,
    conv_weight,
    conv_bias,
    dt_proj,
    dt_bias,
    a_log,
    d_skip,
    gated,
    padded,
    step_buf,
    drive_buf,
    part_buf,
    state,
):
    tokens, width = gated.shape
    states = a_log.shape[0]
    chunk = min(CHUNK, tokens)
    padded[0:8] = jnp.zeros((8, width), jnp.float32)
    state[...] = jnp.zeros_like(state)
    a_scaled = jnp.exp(a_log[...]) * (-1.0 / math.log(2.0))

    def one_chunk(index, _):
        rows = pl.ds(pl.multiple_of(index * chunk, chunk), chunk)
        padded[8 : 8 + chunk] = conv_input[rows, :].astype(jnp.float32)
        convolved = conv_bias[...]
        for tap in range(TAPS):
            start = 8 - (TAPS - 1) + tap
            convolved = convolved + conv_weight[tap : tap + 1, :] * padded[start : start + chunk]
        padded[0:8] = padded[chunk : chunk + 8]
        activated = convolved / (1.0 + jnp.exp(-convolved))
        raw = (
            jnp.dot(step_raw[rows, :], dt_proj[...], preferred_element_type=jnp.float32)
            + dt_bias[...]
        )
        step = jnp.maximum(raw, 0.0) + jnp.log1p(jnp.exp(-jnp.abs(raw)))
        step_buf[...] = step
        drive_buf[...] = step * activated
        b_tile = b_rows[:, rows]
        c_tile = c_rows[:, rows]
        now = state[...]
        for t in range(chunk):
            decay = jnp.exp2(step_buf[t : t + 1, :] * a_scaled)
            now = decay * now + drive_buf[t : t + 1, :] * b_tile[:, t : t + 1]
            seen = now * c_tile[:, t : t + 1]
            total = seen[0:8]
            for block in range(1, states // 8):
                total = total + seen[8 * block : 8 * block + 8]
            part_buf[t] = total
        state[...] = now
        scanned = jnp.sum(part_buf[...], axis=1) + d_skip[...] * activated
        gate_now = gate[rows, :].astype(jnp.float32)
        gated[rows, :] = (scanned * (gate_now / (1.0 + jnp.exp(-gate_now)))).astype(gated.dtype)
        return 0

    lax.fori_loop(0, tokens // chunk, one_chunk, 0)


def run_scan(conv_input, *rest):
    tokens, width = conv_input.shape
    chunk = min(CHUNK, tokens)
    states = rest[-2].shape[0]
    vmem = pl.BlockSpec(memory_space=pltpu.VMEM)
    return pl.pallas_call(
        scan_kernel,
        out_shape=jax.ShapeDtypeStruct((tokens, width), jnp.bfloat16),
        in_specs=[vmem] * (1 + len(rest)),
        out_specs=vmem,
        scratch_shapes=[
            pltpu.VMEM((chunk + 8, width), jnp.float32),
            pltpu.VMEM((chunk, width), jnp.float32),
            pltpu.VMEM((chunk, width), jnp.float32),
            pltpu.VMEM((chunk, 8, width), jnp.float32),
            pltpu.VMEM((states, width), jnp.float32),
        ],
        compiler_params=pltpu.CompilerParams(vmem_limit_bytes=40 * 1024 * 1024),
    )(conv_input, *rest)


def on_device(
    tokens,
    norm_gain,
    in_proj,
    conv_weight,
    conv_bias,
    x_proj,
    dt_proj,
    dt_bias,
    a_log,
    d_skip,
    out_proj,
):
    n_seq, n_ch = lax.axis_size("seq"), lax.axis_size("ch")
    seq = lax.axis_index("seq")
    local_tokens = tokens.shape[0]
    all_tokens = local_tokens * n_seq
    channels = in_proj.shape[2]
    width = channels // n_seq
    rank = dt_proj.shape[0]
    states = a_log.shape[1]

    token_rows = lax.all_gather(tokens, "ch", axis=1, tiled=True)
    tokens_wide = token_rows.astype(jnp.float32)
    scale_rows = lax.rsqrt(jnp.mean(tokens_wide * tokens_wide, axis=-1, keepdims=True) + 1e-06)
    normed = (tokens_wide * scale_rows * norm_gain).astype(jnp.bfloat16)
    columns = lax.all_to_all(normed, "seq", split_axis=1, concat_axis=0, tiled=True)

    conv_part = jnp.dot(
        columns, in_proj[:, 0, :], preferred_element_type=jnp.float32
    ).astype(jnp.bfloat16)
    conv_tokens = lax.psum_scatter(conv_part, "seq", scatter_dimension=0, tiled=True)
    gate_part = jnp.einsum(
        "td,dse->ste",
        columns,
        in_proj[:, 1, :].reshape(-1, n_seq, width),
        preferred_element_type=jnp.float32,
    ).astype(jnp.bfloat16)
    gate = lax.psum_scatter(gate_part, "seq", scatter_dimension=0, tiled=False)

    conv_columns = lax.all_to_all(conv_tokens, "seq", split_axis=1, concat_axis=0, tiled=True)
    earlier = lax.ppermute(
        conv_tokens[-(TAPS - 1) :], "seq", [(i, i + 1) for i in range(n_seq - 1)]
    )
    padded = jnp.concatenate([earlier, conv_tokens], 0).astype(jnp.float32)
    convolved = conv_bias
    for tap in range(TAPS):
        convolved = convolved + conv_weight[tap] * padded[tap : tap + local_tokens]
    activated_half = jax.nn.silu(convolved).astype(jnp.bfloat16)
    features = lax.psum(
        jnp.dot(activated_half, x_proj, preferred_element_type=jnp.float32), "ch"
    )
    tail = features[:, rank:]
    high = lax.reduce_precision(tail, 8, 7)
    sent = jnp.concatenate([features[:, :rank], high, tail - high], 1).astype(jnp.bfloat16)
    everyone = lax.all_gather(sent, "seq", axis=0, tiled=True)
    step_raw = everyone[:, :rank]
    pair = everyone[:, rank:].astype(jnp.float32)
    bc_rows = (pair[:, : 2 * states] + pair[:, 2 * states :]).T

    def mine(array, axis):
        return lax.dynamic_slice_in_dim(array, seq * width, width, axis)

    gated = run_scan(
        conv_columns,
        gate,
        step_raw,
        bc_rows[:states],
        bc_rows[states:],
        mine(conv_weight, 1),
        mine(conv_bias, 0)[None],
        mine(dt_proj, 1),
        mine(dt_bias, 0)[None],
        mine(a_log, 0).T,
        mine(d_skip, 0)[None],
    )
    gated_all = lax.all_gather(gated, "seq", axis=1, tiled=True)
    partial_out = jnp.dot(gated_all, out_proj, preferred_element_type=jnp.float32).astype(
        jnp.bfloat16
    )
    summed = lax.psum_scatter(partial_out, "ch", scatter_dimension=0, tiled=True)
    share = n_seq // n_ch
    out_width = out_proj.shape[1]
    blocks = summed.reshape(share, local_tokens, out_width)
    mixed = jnp.zeros((local_tokens, share, out_width), jnp.bfloat16)
    for turn in range(share):
        route = [
            (s * n_ch + c, (share * c + (s + turn) % share) * n_ch + s // share)
            for s in range(n_seq)
            for c in range(n_ch)
        ]
        block = lax.dynamic_index_in_dim(blocks, (seq + turn) % share, 0, keepdims=False)
        arrived = lax.ppermute(block, ("seq", "ch"), route)
        mixed = lax.dynamic_update_slice_in_dim(
            mixed, arrived[:, None], (seq - turn + share) % share, 1
        )
    return mixed.reshape(local_tokens, share * out_width)


def solution(mesh):
    placed = (
        P("seq", "ch"),
        P(),
        P("seq", None, "ch"),
        P(None, "ch"),
        P("ch"),
        P("ch", None),
        P(None, "ch"),
        P("ch"),
        P("ch", None),
        P("ch"),
        P("ch", "seq"),
    )
    return jax.shard_map(
        on_device, mesh=mesh, in_specs=placed, out_specs=P("seq", "ch"), check_vma=False
    )
```

time: 1040 us -> 493 us (0.47)
  waiting for transfers between devices: 762 us -> 370 us
  other arithmetic: 92.4 us -> 6.6 us
  starting transfers between devices: 56.5 us -> 22.3 us
  local copies, waits for them, and re-layouts: 73.9 us -> 47.4 us
  Pallas kernels: 0 us -> 10.7 us
    all_gather x2, waiting for transfers between devices: 632 us -> 96.9 us  [the longest x1 74.9 us: on_device(): gated_all = lax.all_gather(gated, 'seq', axis=1, tiled=True)]
    reduce_scatter x1 -> x3, waiting for transfers between devices: 56.6 us -> 195 us  [the longest x1 87.2 us: on_device(): lax.psum_scatter(conv_part, 'seq', scatter_dimension=0, tiled=True)]
    another operation x32 -> x1, other arithmetic: 55.9 us -> 0.72 us  [the longest x16 54.1 us: block_scan(): jnp.cumsum(jnp.exp(-running_log) * driven, axis=1)]
    ppermute x8 -> x3, starting transfers between devices: 56.2 us -> 10.3 us  [the longest x2 6.93 us: on_device(): arrived = lax.ppermute(block, ('seq', 'ch'), route)]
    reduce_sum x32 -> x0, other arithmetic: 26.8 us -> none  [the longest x16 20.4 us: block_scan(): jnp.sum(full_states * c_sub, axis=2).reshape(local_tokens, block_width)]
    mul x48 -> x0, local copies, waits for them, and re-layouts: 22.5 us -> none  [the longest x16 11.3 us: block_scan(): step_block[:, None, :] * a_block[None]]
    ppermute x8 -> x3, waiting for transfers between devices: 32 us -> 11.5 us  [the longest x2 10.1 us: on_device(): arrived = lax.ppermute(block, ('seq', 'ch'), route)]
    all_to_all x0 -> x2, waiting for transfers between devices: none -> 16.2 us  [the longest x1 16.2 us: on_device(): lax.all_to_all(normed, 'seq', split_axis=1, concat_axis=0, tiled=True)]
  transfers between devices with their start and end apart: 13 -> 12, of which waited for: 12 -> 11; matrix products, arithmetic and copies ran while one was open for 16% -> 8% of each run, Pallas kernels for 0% -> 0%
where the time goes in v1:
time: 493 us; the launch traced here: 492 us
  waiting for transfers between devices  370 us (75%)
  local copies, waits for them, and re-layouts  47.4 us (10%)
  starting transfers between devices  22.3 us (5%)
  matrix products  20.7 us (4%)
  between operations  13.7 us (3%)
  Pallas kernels  10.7 us (2%)
  other arithmetic  6.6 us (1%)
    reduce_scatter x1, waiting for transfers between devices, on_device(): lax.psum_scatter(conv_part, 'seq', scatter_dimension=0, tiled=True)  87.2 us
    reduce_scatter x1, waiting for transfers between devices, on_device(): gate = lax.psum_scatter(gate_part, 'seq', scatter_dimension=0, tiled=False)  85.7 us
    all_gather x1, waiting for transfers between devices, on_device(): gated_all = lax.all_gather(gated, 'seq', axis=1, tiled=True)  74.9 us
    psum x1, waiting for transfers between devices, on_device(): lax.psum(jnp.dot(activated_half, x_proj, preferred_element_type=jnp.float...  31.4 us
    reduce_scatter x1, waiting for transfers between devices, on_device(): lax.psum_scatter(partial_out, 'ch', scatter_dimension=0, tiled=True)  22.1 us
    all_gather x1, waiting for transfers between devices, on_device(): everyone = lax.all_gather(sent, 'seq', axis=0, tiled=True)  22 us
    all_gather x1, waiting for transfers between devices, on_device(): token_rows = lax.all_gather(tokens, 'ch', axis=1, tiled=True)  18.5 us
    unnamed x26, local copies, waits for them, and re-layouts  17.5 us
  transfers between devices with their start and end apart: 12, of which 11 were waited for; matrix products, arithmetic and copies ran while one was open for 8% of the time, Pallas kernels for 0%

profile of v1, /device:TPU:2, one launch (start us, length us, event | category | flops | bytes accessed | tf_op | source)
XLA Modules:
  0.0 491.6 jit_solution(14177500883254940508)
XLA Ops:
  7.3 18.5 %all-gather.4.cloned.1.call-done = bf16[128,4096]{1,0:T(8,128)(2,1)} async-done(((bf16[128,1024]{1,0:T(8,128)(2,1)}), bf16[128,4096]{1,0:T(8,128)(2,1)}) %all-gather.4.cloned.1.call-update) | async-done | bytes 1048592 | tf_op jit(solution)/shard_map/all_gather | solution.py:120
  25.8 1.5 fusion
  27.3 1.6 fusion.2
  30.0 5.8 %all-to-all-start = ((bf16[128,8,512]{2,0,1:T(8,128)(2,1)}), bf16[128,8,512]{2,0,1:T(8,128)(2,1)S(1)}, u32[]{:S(2)}, u32[]{:S(2)}) async-start(bf16[128,8,512]{2,0,1:T(8,128)(2,1)} %bitcast.47), calls=%async_computation | async-start | bytes 2097152 | tf_op jit(solution)/shard_map/all_to_all | solution.py:124
  35.8 9.9 %fusion.11 = (bf16[512,1,2048]{2,1,0:T(2,128)(2,1)}, bf16[512,1,2048]{2,1,0:T(2,128)(2,1)}) fusion(bf16[512,2,2048]{2,1,0:T(2,128)(2,1)} %param.13), kind=kLoop, calls=%fused_computation.37 | loop fusion | bytes 8388608 | tf_op jit(solution)/shard_map/slice | solution.py:133
  45.7 16.2 %all-to-all-done = bf16[128,8,512]{2,0,1:T(8,128)(2,1)S(1)} async-done(((bf16[128,8,512]{2,0,1:T(8,128)(2,1)}), bf16[128,8,512]{2,0,1:T(8,128)(2,1)S(1)}, u32[]{:S(2)}, u32[]{:S(2)}) %all-to-all-start) | async-done | bytes 1048608 | tf_op jit(solution)/shard_map/all_to_all | solution.py:124
  61.9 6.7 %convolution_convert_fusion = bf16[1024,2048]{1,0:T(8,128)(2,1)} fusion(bf16[1024,512]{1,0:T(8,128)(2,1)S(1)} %bitcast.56, bf16[512,1,2048]{2,1,0:T(2,128)(2,1)} %get-tuple-element.6), kind=kOutput, calls=%fused_computation.1 | convolution fusion | flops 2149580800 | bytes 7340032 | tf_op jit(solution)/shard_map/dot_general | solution.py:126
  68.7 87.2 %reduce-scatter.4.cloned.1.call-done = bf16[128,2048]{1,0:T(8,128)(2,1)} async-done(((bf16[1024,2048]{1,0:T(8,128)(2,1)}), bf16[128,2048]{1,0:T(8,128)(2,1)}) %reduce-scatter.4.cloned.1.call-update) | async-done | bytes 524304 | tf_op jit(solution)/shard_map/reduce_scatter | solution.py:129
  156.6 3.4 collective-permute-start
  160.0 1.4 collective-permute-done
  161.4 1.2 maximum_convert_fusion
  162.6 1.9 fusion.7
  164.6 31.4 %all-reduce.2.cloned.1.call-done = f32[128,544]{0,1:T(8,128)} async-done(((f32[128,544]{0,1:T(8,128)}), f32[128,544]{0,1:T(8,128)}) %all-reduce.2.cloned.1.call-update) | async-done | bytes 278544 | tf_op jit(solution)/shard_map/psum | solution.py:147
  198.5 10.5 %copy.25 = bf16[512,1,2048]{0,2,1:T(8,128)(2,1)} copy(bf16[512,1,2048]{2,1,0:T(2,128)(2,1)} %get-tuple-element.5) | data formatting | bytes 4194304
  209.0 5.9 %convert_bitcast_fusion = bf16[8,1024,256]{2,1,0:T(8,128)(2,1)} fusion(bf16[1024,512,1]{1,0,2:T(8,128)(2,1)S(1)} %bitcast.57, bf16[512,8,256]{0,2,1:T(8,128)(2,1)} %bitcast.55), kind=kOutput, calls=%fused_computation | convolution fusion | flops 2149580800 | bytes 7340032 | tf_op jit(solution)/shard_map/td,dse->ste/dot_general | solution.py:130
  215.6 1.3 dynamic_slice.28
  217.0 1.3 dynamic_slice.30
  219.9 6.0 %all-to-all-start.1 = ((bf16[128,8,256]{2,0,1:T(8,128)(2,1)}), bf16[128,8,256]{2,0,1:T(8,128)(2,1)}, u32[]{:S(2)}, u32[]{:S(2)}) async-start(bf16[128,8,256]{2,0,1:T(8,128)(2,1)} %bitcast.48), calls=%async_computation.2 | async-start | bytes 1048576 | tf_op jit(solution)/shard_map/all_to_all | solution.py:138
  227.5 22.0 %all-gather.6.cloned.1.call-done = bf16[1024,576]{0,1:T(8,128)(2,1)} async-done(((bf16[128,576]{0,1:T(8,128)(2,1)}), bf16[1024,576]{0,1:T(8,128)(2,1)}) %all-gather.6.cloned.1.call-update) | async-done | bytes 1179664 | tf_op jit(solution)/shard_map/all_gather | solution.py:153
  249.5 2.3 slice.84
  251.8 1.5 copy.20.step_raw
  254.9 85.7 %reduce-scatter.6.cloned.1.call-done = bf16[1,1024,256]{2,1,0:T(8,128)(2,1)} async-done(((bf16[8,1024,256]{2,1,0:T(8,128)(2,1)}), bf16[1,1024,256]{2,1,0:T(8,128)(2,1)}) %reduce-scatter.6.cloned.1.call-update) | async-done | bytes 524304 | tf_op jit(solution)/shard_map/reduce_scatter | solution.py:136
  346.0 10.7 %shard_map.109 = bf16[1024,256]{1,0:T(8,128)(2,1)S(1)} custom-call(bf16[1024,256]{1,0:T(8,128)(2,1)} %bitcast.4.conv_input, bf16[1024,256]{1,0:T(8,128)(2,1)S(1)} %bitcast.49, bf16[1024,512]{1,0:T(8,128)(2,1)S(1)} %copy.20.step_raw, f32[16,1024]{1,0:T(8,128)S(1)} %copy-done.4, f32[16,1024]{1,0:T(8,128)S(1)} %copy-done.3, f32[4,256]{1,0:T(4,128)S(1)} %copy-done.5, ...), custom_call_target="tpu_custom_call" | custom-call | tf_op jit(solution)/shard_map/pallas_call | solution.py:82
  357.6 74.9 %all-gather.8.cloned.1.call-done = bf16[1024,2048]{1,0:T(8,128)(2,1)} async-done(((bf16[1024,256]{1,0:T(8,128)(2,1)}), bf16[1024,2048]{1,0:T(8,128)(2,1)}) %all-gather.8.cloned.1.call-update) | async-done | bytes 4194320 | tf_op jit(solution)/shard_map/all_gather | solution.py:174
  432.5 6.2 %convolution_convert_fusion.1 = bf16[1024,512]{1,0:T(8,128)(2,1)} fusion(bf16[1024,2048]{1,0:T(8,128)(2,1)} %all-gather.8.cloned.1.call-done, bf16[2048,512]{1,0:T(8,128)(2,1)} %param.21), kind=kOutput, calls=%fused_computation.8 | convolution fusion | flops 2148007936 | bytes 7340032 | tf_op jit(solution)/shard_map/dot_general | solution.py:175
  438.8 22.1 %reduce-scatter.8.cloned.1.call-done = bf16[256,512]{1,0:T(8,128)(2,1)} async-done(((bf16[1024,512]{1,0:T(8,128)(2,1)}), bf16[256,512]{1,0:T(8,128)(2,1)}) %reduce-scatter.8.cloned.1.call-update) | async-done | bytes 262160 | tf_op jit(solution)/shard_map/reduce_scatter | solution.py:178
  461.8 4.5 collective-permute-start.2
  466.3 2.4 collective-permute-start.1
  468.8 6.4 %collective-permute-done.2 = bf16[128,512]{1,0:T(8,128)(2,1)S(1)} collective-permute-done((bf16[128,512]{1,0:T(8,128)(2,1)S(1)}, bf16[128,512]{1,0:T(8,128)(2,1)S(1)}, u32[]{:S(2)}, u32[]{:S(2)}) %collective-permute-start.2) | collective-permute-done | bytes 131104 | tf_op jit(solution)/shard_map/ppermute | solution.py:190
  475.4 3.7 collective-permute-done.1
  479.4 2.3 dynamic_update_slice.6
  481.7 2.3 dynamic_update_slice.7
  (59 shorter events, 19.2 us)
Async XLA Ops:
  6.5 156.1 %copy-start = (bf16[2048,544]{0,1:T(8,128)(2,1)S(1)}, bf16[2048,544]{0,1:T(8,128)(2,1)}, u32[]{:S(2)}) copy-start(bf16[2048,544]{0,1:T(8,128)(2,1)} %param.16) | copy-start | bytes 6684676
  6.5 19.2 %all-gather.4.cloned.1.call-start = ((), (), s32[]{:S(2)}) async-start(), calls=%async_computation.5 | async-start | bytes 1310720 | tf_op jit(solution)/shard_map/all_gather | solution.py:120
  30.0 31.9 %all-to-all-start = ((bf16[128,8,512]{2,0,1:T(8,128)(2,1)}), bf16[128,8,512]{2,0,1:T(8,128)(2,1)S(1)}, u32[]{:S(2)}, u32[]{:S(2)}) async-start(bf16[128,8,512]{2,0,1:T(8,128)(2,1)} %bitcast.47), calls=%async_computation | async-start | bytes 2097152 | tf_op jit(solution)/shard_map/all_to_all | solution.py:124
  35.7 120.1 %reduce-scatter.4.cloned.1.call-start = ((), (), s32[]{:S(2)}) async-start(), calls=%async_computation.6 | async-start | bytes 4718592 | tf_op jit(solution)/shard_map/reduce_scatter | solution.py:129
  68.6 91.4 %copy-start.10 = (f32[4,2048]{1,0:T(4,128)S(1)}, f32[4,2048]{1,0:T(4,128)}, u32[]{:S(2)}) copy-start(f32[4,2048]{1,0:T(4,128)} %param.14) | copy-start | bytes 98308
  68.6 94.0 %copy-start.11 = (f32[2048]{0:T(1024)S(1)}, f32[2048]{0:T(1024)}, u32[]{:S(2)}) copy-start(f32[2048]{0:T(1024)} %param.15) | copy-start | bytes 24580
  68.6 127.5 %all-reduce.2.cloned.1.call-start = ((), (), s32[]{:S(2)}) async-start(), calls=%async_computation.8 | async-start | bytes 557056 | tf_op jit(solution)/shard_map/psum | solution.py:147
  156.6 4.8 collective-permute-start
  164.6 84.9 %all-gather.6.cloned.1.call-start = ((), (), s32[]{:S(2)}) async-start(), calls=%async_computation.9 | async-start | bytes 1327104 | tf_op jit(solution)/shard_map/all_gather | solution.py:153
  198.4 142.2 %reduce-scatter.6.cloned.1.call-start = ((), (), s32[]{:S(2)}) async-start(), calls=%async_computation.7 | async-start | bytes 4718592 | tf_op jit(solution)/shard_map/reduce_scatter | solution.py:136
  215.0 4.1 copy-start.9
  219.9 120.7 %all-to-all-start.1 = ((bf16[128,8,256]{2,0,1:T(8,128)(2,1)}), bf16[128,8,256]{2,0,1:T(8,128)(2,1)}, u32[]{:S(2)}, u32[]{:S(2)}) async-start(bf16[128,8,256]{2,0,1:T(8,128)(2,1)} %bitcast.48), calls=%async_computation.2 | async-start | bytes 1048576 | tf_op jit(solution)/shard_map/all_to_all | solution.py:138
  225.9 206.6 %all-gather.8.cloned.1.call-start = ((), (), s32[]{:S(2)}) async-start(), calls=%async_computation.10 | async-start | bytes 4718592 | tf_op jit(solution)/shard_map/all_gather | solution.py:174
  340.6 1.0 copy-start.2
  341.7 0.8 copy-start.3
  342.5 0.8 copy-start.4
  343.3 0.7 copy-start.5
  344.0 0.7 copy-start.6
  344.7 0.7 copy-start.7
  345.3 0.7 copy-start.8
  356.7 0.8 copy-start.1
  357.6 103.2 %reduce-scatter.8.cloned.1.call-start = ((), (), s32[]{:S(2)}) async-start(), calls=%async_computation.11 | async-start | bytes 1310720 | tf_op jit(solution)/shard_map/reduce_scatter | solution.py:178
  461.8 13.4 %collective-permute-start.2 = (bf16[128,512]{1,0:T(8,128)(2,1)S(1)}, bf16[128,512]{1,0:T(8,128)(2,1)S(1)}, u32[]{:S(2)}, u32[]{:S(2)}) collective-permute-start(bf16[128,512]{1,0:T(8,128)(2,1)S(1)} %get-tuple-element.9), channel_id=1, source_target_pairs={{0,4},{1,12},{2,20},{3,28},{4,0},{5,8},{6,16},{7,24},{8,5},{9,13},... | collective-permute-start | bytes 393224 | tf_op jit(solution)/shard_map/ppermute | solution.py:190
  466.3 12.7 %collective-permute-start.1 = (bf16[128,512]{1,0:T(8,128)(2,1)S(1)}, bf16[128,512]{1,0:T(8,128)(2,1)S(1)}, u32[]{:S(2)}, u32[]{:S(2)}) collective-permute-start(bf16[128,512]{1,0:T(8,128)(2,1)S(1)} %get-tuple-element.10), channel_id=1, source_target_pairs={{0,0},{1,8},{2,16},{3,24},{4,4},{5,12},{6,20},{7,28},{8,1},{9,9},{... | collective-permute-start | bytes 393224 | tf_op jit(solution)/shard_map/ppermute | solution.py:190
Sparse Core Ops, SparseCore 0:
  8.9 16.7 all-gather.3
  68.7 87.0 reduce-scatter.3
  164.7 31.3 all-reduce.1
  198.6 50.8 all-gather.5
  253.4 87.1 reduce-scatter.5
  357.7 74.7 all-gather.7
  438.9 21.9 reduce-scatter.7

commit v2 on v1

--- a/solution.py
+++ b/solution.py
@@ -95,6 +95,185 @@
     )(conv_input, *rest)
 
 
+def ring_place(n):
+    me = lax.axis_index("seq")
+    along, across = lax.div(me, 2), lax.rem(me, 2)
+    place = along + across * (n - 1 - 2 * along)
+
+    def index_at(q):
+        q = lax.rem(q, n)
+        far = lax.div(q, n // 2)
+        return 2 * (q + far * (n - 1 - 2 * q)) + far
+
+    return place, index_at
+
+
+def greet(targets):
+    barrier = pltpu.get_barrier_semaphore()
+    for target in targets:
+        pl.semaphore_signal(
+            barrier, inc=1, device_id={"seq": target}, device_id_type=pl.DeviceIdType.MESH
+        )
+    pl.semaphore_wait(barrier, len(targets))
+
+
+def push(slots, way, step, target, send_sem, recv_sem):
+    return pltpu.make_async_remote_copy(
+        src_ref=slots.at[way, step],
+        dst_ref=slots.at[way, step + 1],
+        send_sem=send_sem.at[way, step],
+        recv_sem=recv_sem.at[way, step],
+        device_id={"seq": target},
+        device_id_type=pl.DeviceIdType.MESH,
+    )
+
+
+def project_kernel(
+    n,
+    columns,
+    w_conv,
+    w_gate,
+    conv_out,
+    gate_out,
+    conv_slots,
+    gate_slots,
+    conv_next,
+    gate_next,
+    conv_send,
+    conv_recv,
+    gate_send,
+    gate_recv,
+):
+    place, index_at = ring_place(n)
+    targets = (index_at(place + 1), index_at(place + n - 1))
+    local, half = conv_slots.shape[2:]
+    rows_half = gate_slots.shape[2]
+    greet(targets)
+
+    def products(way, q):
+        owner = index_at(q)
+        rows = pl.ds(pl.multiple_of(owner * local, local), local)
+        conv_next[way] = jnp.dot(
+            columns[rows, :],
+            w_conv[:, way * half : (way + 1) * half],
+            preferred_element_type=jnp.float32,
+        )
+        gate_next[way] = jnp.dot(
+            columns[way * rows_half : (way + 1) * rows_half, :],
+            w_gate[owner],
+            preferred_element_type=jnp.float32,
+        )
+
+    for way in range(2):
+        products(way, place + (n - 1 if way == 0 else 1))
+        conv_slots[way, 0] = conv_next[way].astype(jnp.bfloat16)
+        gate_slots[way, 0] = gate_next[way].astype(jnp.bfloat16)
+
+    def turn(step, _):
+        copies = []
+        for way in range(2):
+            copies.append(push(conv_slots, way, step, targets[way], conv_send, conv_recv))
+            copies.append(push(gate_slots, way, step, targets[way], gate_send, gate_recv))
+        for copy in copies:
+            copy.start()
+        for way in range(2):
+            products(way, place + (2 * n - 2 - step if way == 0 else 2 + step))
+        for copy in copies:
+            copy.wait()
+        for way in range(2):
+            conv_slots[way, step + 1] = (
+                conv_slots[way, step + 1].astype(jnp.float32) + conv_next[way]
+            ).astype(jnp.bfloat16)
+            gate_slots[way, step + 1] = (
+                gate_slots[way, step + 1].astype(jnp.float32) + gate_next[way]
+            ).astype(jnp.bfloat16)
+        return 0
+
+    lax.fori_loop(0, n - 1, turn, 0)
+    for way in range(2):
+        conv_out[:, way * half : (way + 1) * half] = conv_slots[way, n - 1]
+        gate_out[way * rows_half : (way + 1) * rows_half, :] = gate_slots[way, n - 1]
+
+
+def project(columns, w_conv, w_gate):
+    n, _, width = w_gate.shape
+    total, channels = columns.shape[0], w_conv.shape[1]
+    local, half = total // n, channels // 2
+    vmem = pl.BlockSpec(memory_space=pltpu.VMEM)
+    return pl.pallas_call(
+        functools.partial(project_kernel, n),
+        out_shape=(
+            jax.ShapeDtypeStruct((local, channels), jnp.bfloat16),
+            jax.ShapeDtypeStruct((total, width), jnp.bfloat16),
+        ),
+        in_specs=[vmem] * 3,
+        out_specs=(vmem, vmem),
+        scratch_shapes=[
+            pltpu.VMEM((2, n, local, half), jnp.bfloat16),
+            pltpu.VMEM((2, n, total // 2, width), jnp.bfloat16),
+            pltpu.VMEM((2, local, half), jnp.float32),
+            pltpu.VMEM((2, total // 2, width), jnp.float32),
+        ]
+        + [pltpu.SemaphoreType.DMA((2, n - 1))] * 4,
+        compiler_params=pltpu.CompilerParams(
+            collective_id=0, has_side_effects=True, vmem_limit_bytes=56 * 1024 * 1024
+        ),
+    )(columns, w_conv, w_gate)
+
+
+def gather_kernel(n, gated, weights, out, slots, totals, send_sem, recv_sem):
+    place, index_at = ring_place(n)
+    targets = (index_at(place + 1), index_at(place + n - 1))
+    rows_half = slots.shape[2]
+    greet(targets)
+
+    def add(way, step):
+        owner = index_at(place + (n - step if way == 0 else step))
+        totals[way] += jnp.dot(
+            slots[way, step], weights[owner], preferred_element_type=jnp.float32
+        )
+
+    for way in range(2):
+        slots[way, 0] = gated[way * rows_half : (way + 1) * rows_half, :]
+    totals[...] = jnp.zeros_like(totals)
+
+    def turn(step, _):
+        copies = [push(slots, way, step, targets[way], send_sem, recv_sem) for way in range(2)]
+        for copy in copies:
+            copy.start()
+        for way in range(2):
+            add(way, step)
+        for copy in copies:
+            copy.wait()
+        return 0
+
+    lax.fori_loop(0, n - 1, turn, 0)
+    for way in range(2):
+        add(way, n - 1)
+        out[way * rows_half : (way + 1) * rows_half, :] = totals[way].astype(out.dtype)
+
+
+def gather_project(gated, weights):
+    n, width, out_width = weights.shape
+    total = gated.shape[0]
+    vmem = pl.BlockSpec(memory_space=pltpu.VMEM)
+    return pl.pallas_call(
+        functools.partial(gather_kernel, n),
+        out_shape=jax.ShapeDtypeStruct((total, out_width), jnp.bfloat16),
+        in_specs=[vmem] * 2,
+        out_specs=vmem,
+        scratch_shapes=[
+            pltpu.VMEM((2, n, total // 2, width), jnp.bfloat16),
+            pltpu.VMEM((2, total // 2, out_width), jnp.float32),
+            pltpu.SemaphoreType.DMA((2, n - 1)),
+            pltpu.SemaphoreType.DMA((2, n - 1)),
+        ],
+        compiler_params=pltpu.CompilerParams(
+            collective_id=1, has_side_effects=True, vmem_limit_bytes=56 * 1024 * 1024
+        ),
+    )(gated, weights)
+
+
 def on_device(
     tokens,
     norm_gain,
@@ -123,17 +302,8 @@
     normed = (tokens_wide * scale_rows * norm_gain).astype(jnp.bfloat16)
     columns = lax.all_to_all(normed, "seq", split_axis=1, concat_axis=0, tiled=True)
 
-    conv_part = jnp.dot(
-        columns, in_proj[:, 0, :], preferred_element_type=jnp.float32
-    ).astype(jnp.bfloat16)
-    conv_tokens = lax.psum_scatter(conv_part, "seq", scatter_dimension=0, tiled=True)
-    gate_part = jnp.einsum(
-        "td,dse->ste",
-        columns,
-        in_proj[:, 1, :].reshape(-1, n_seq, width),
-        preferred_element_type=jnp.float32,
-    ).astype(jnp.bfloat16)
-    gate = lax.psum_scatter(gate_part, "seq", scatter_dimension=0, tiled=False)
+    w_gate = in_proj[:, 1, :].reshape(-1, n_seq, width).transpose(1, 0, 2)
+    conv_tokens, gate = project(columns, in_proj[:, 0, :], w_gate)
 
     conv_columns = lax.all_to_all(conv_tokens, "seq", split_axis=1, concat_axis=0, tiled=True)
     earlier = lax.ppermute(
@@ -171,10 +341,7 @@
         mine(a_log, 0).T,
         mine(d_skip, 0)[None],
     )
-    gated_all = lax.all_gather(gated, "seq", axis=1, tiled=True)
-    partial_out = jnp.dot(gated_all, out_proj, preferred_element_type=jnp.float32).astype(
-        jnp.bfloat16
-    )
+    partial_out = gather_project(gated, out_proj.reshape(n_seq, width, -1))
     summed = lax.psum_scatter(partial_out, "ch", scatter_dimension=0, tiled=True)
     share = n_seq // n_ch
     out_width = out_proj.shape[1]

time: 493 us -> 378 us (0.77)
  waiting for transfers between devices: 370 us -> 123 us
  Pallas kernels: 10.7 us -> 153 us
  matrix products: 20.7 us -> 1.87 us
  local copies, waits for them, and re-layouts: 47.4 us -> 56.7 us
    reduce_scatter x2 -> x0, waiting for transfers between devices: 173 us -> none  [the longest x1 87.2 us: on_device(): lax.psum_scatter(conv_part, 'seq', scatter_dimension=0, tiled=True)]
    pallas_call x0 -> x2, Pallas kernels: none -> 143 us  [the longest x1 89.2 us: project(): pl.pallas_call(functools.partial(project_kernel, n), out_shape=(jax.Shape...]
    all_gather x1 -> x0, waiting for transfers between devices: 74.9 us -> none  [on_device(): gated_all = lax.all_gather(gated, 'seq', axis=1, tiled=True)]
    dot_general x3 -> x0, matrix products: 18.8 us -> none  [the longest x1 6.68 us: on_device(): jnp.dot(columns, in_proj[:, 0, :], preferred_element_type=jnp.float32)]
    all_to_all x1, waiting for transfers between devices: 16.2 us -> 0.01 us  [on_device(): lax.all_to_all(normed, 'seq', split_axis=1, concat_axis=0, tiled=True)]
    all_gather x1, waiting for transfers between devices: 22 us -> 36.2 us  [on_device(): everyone = lax.all_gather(sent, 'seq', axis=0, tiled=True)]
    unnamed x26 -> x29, local copies, waits for them, and re-layouts: 17.5 us -> 23.2 us
  transfers between devices with their start and end apart: 12 -> 9, of which waited for: 11 -> 7; matrix products, arithmetic and copies ran while one was open for 8% -> 11% of each run, Pallas kernels for 0% -> 0%
where the time goes in v2:
time: 378 us; the launch traced here: 377 us
  Pallas kernels  153 us (40%)
  waiting for transfers between devices  123 us (33%)
  local copies, waits for them, and re-layouts  56.7 us (15%)
  starting transfers between devices  21.6 us (6%)
  between operations  13.3 us (4%)
  other arithmetic  6.6 us (2%)
    pallas_call x1, Pallas kernels, project(): pl.pallas_call(functools.partial(project_kernel, n), out_shape=(jax.Shape...  89.2 us
    pallas_call x1, Pallas kernels, gather_project(): pl.pallas_call(functools.partial(gather_kernel, n), out_shape=jax.ShapeDt...  53.5 us
    all_gather x1, waiting for transfers between devices, on_device(): everyone = lax.all_gather(sent, 'seq', axis=0, tiled=True)  36.2 us
    psum x1, waiting for transfers between devices, on_device(): lax.psum(jnp.dot(activated_half, x_proj, preferred_element_type=jnp.float...  31.6 us
    unnamed x29, local copies, waits for them, and re-layouts  23.2 us
    reduce_scatter x1, waiting for transfers between devices, on_device(): lax.psum_scatter(partial_out, 'ch', scatter_dimension=0, tiled=True)  22.9 us
    all_gather x1, waiting for transfers between devices, on_device(): token_rows = lax.all_gather(tokens, 'ch', axis=1, tiled=True)  18.5 us
    ppermute x2, waiting for transfers between devices, on_device(): arrived = lax.ppermute(block, ('seq', 'ch'), route)  11.9 us
  transfers between devices with their start and end apart: 9, of which 7 were waited for; matrix products, arithmetic and copies ran while one was open for 11% of the time, Pallas kernels for 0%

profile of v2, /device:TPU:2, one launch (start us, length us, event | category | flops | bytes accessed | tf_op | source)
XLA Modules:
  0.0 376.8 jit_solution(9513469396771984842)
XLA Ops:
  7.3 18.5 %all-gather.3.cloned.1.call-done = bf16[128,4096]{1,0:T(8,128)(2,1)} async-done(((bf16[128,1024]{1,0:T(8,128)(2,1)}), bf16[128,4096]{1,0:T(8,128)(2,1)}) %all-gather.3.cloned.1.call-update) | async-done | bytes 1048592 | tf_op jit(solution)/shard_map/all_gather | solution.py:299
  25.8 1.5 fusion
  27.3 1.6 fusion.2
  28.8 1.1 copy.33
  29.9 5.8 %all-to-all-start = ((bf16[128,8,512]{2,0,1:T(8,128)(2,1)}), bf16[128,8,512]{2,0,1:T(8,128)(2,1)S(1)}, u32[]{:S(2)}, u32[]{:S(2)}) async-start(bf16[128,8,512]{2,0,1:T(8,128)(2,1)} %bitcast.49), calls=%async_computation | async-start | bytes 2097152 | tf_op jit(solution)/shard_map/all_to_all | solution.py:303
  35.7 9.9 %fusion.11 = (bf16[512,1,2048]{2,1,0:T(2,128)(2,1)}, bf16[512,1,2048]{2,1,0:T(2,128)(2,1)}) fusion(bf16[512,2,2048]{2,1,0:T(2,128)(2,1)} %param.13), kind=kLoop, calls=%fused_computation.34 | loop fusion | bytes 8388608 | tf_op jit(solution)/shard_map/slice | solution.py:305
  45.6 10.5 %copy.25 = bf16[512,1,2048]{0,2,1:T(8,128)(2,1)} copy(bf16[512,1,2048]{2,1,0:T(2,128)(2,1)} %get-tuple-element.9) | data formatting | bytes 4194304
  56.1 3.9 %copy.19 = bf16[512,8,256]{2,0,1:T(8,128)(2,1)} copy(bf16[512,8,256]{0,2,1:T(8,128)(2,1)} %bitcast.45) | data formatting | bytes 4194304 | tf_op jit(solution)/shard_map/reshape;squeeze | solution.py:305
  60.0 4.9 %copy.32 = bf16[512,1,2048]{2,0,1:T(8,128)(2,1)} copy(bf16[512,1,2048]{2,1,0:T(2,128)(2,1)} %get-tuple-element.10) | data formatting | bytes 4194304
  64.9 1.0 copy-done.9
  65.9 89.2 %shard_map.109 = (bf16[128,2048]{1,0:T(8,128)(2,1)}, bf16[1024,256]{1,0:T(8,128)(2,1)}) custom-call(bf16[1024,512]{1,0:T(8,128)(2,1)} %bitcast.47, bf16[512,2048]{1,0:T(8,128)(2,1)} %bitcast.44, bf16[8,512,256]{2,1,0:T(8,128)(2,1)} %bitcast.46), custom_call_target="tpu_custom_call" | custom-call | tf_op jit(solution)/shard_map/pallas_call | solution.py:203
  155.9 2.8 collective-permute-start
  158.7 1.4 collective-permute-done
  160.1 1.2 maximum_convert_fusion
  161.3 1.9 fusion.7
  163.2 31.6 %all-reduce.2.cloned.1.call-done = f32[128,544]{0,1:T(8,128)} async-done(((f32[128,544]{0,1:T(8,128)}), f32[128,544]{0,1:T(8,128)}) %all-reduce.2.cloned.1.call-update) | async-done | bytes 278544 | tf_op jit(solution)/shard_map/psum | solution.py:317
  197.9 1.3 dynamic_slice.28
  199.2 1.3 dynamic_slice.30
  202.1 6.0 %all-to-all-start.1 = ((bf16[128,8,256]{2,0,1:T(8,128)(2,1)}), bf16[128,8,256]{2,0,1:T(8,128)(2,1)}, u32[]{:S(2)}, u32[]{:S(2)}) async-start(bf16[128,8,256]{2,0,1:T(8,128)(2,1)} %bitcast.40), calls=%async_computation.1 | async-start | bytes 1048576 | tf_op jit(solution)/shard_map/all_to_all | solution.py:308
  209.7 36.2 %all-gather.5.cloned.1.call-done = bf16[1024,576]{0,1:T(8,128)(2,1)} async-done(((bf16[128,576]{0,1:T(8,128)(2,1)}), bf16[1024,576]{0,1:T(8,128)(2,1)}) %all-gather.5.cloned.1.call-update) | async-done | bytes 1179664 | tf_op jit(solution)/shard_map/all_gather | solution.py:323
  245.8 2.3 slice.83
  248.1 1.5 copy.21.step_raw
  251.2 1.0 copy-done.2
  256.5 10.7 %shard_map.110.gated = bf16[1024,256]{1,0:T(8,128)(2,1)S(1)} custom-call(bf16[1024,256]{1,0:T(8,128)(2,1)} %bitcast.6.conv_input, bf16[1024,256]{1,0:T(8,128)(2,1)S(1)} %copy-done.2, bf16[1024,512]{1,0:T(8,128)(2,1)S(1)} %copy.21.step_raw, f32[16,1024]{1,0:T(8,128)S(1)} %copy-done.4, f32[16,1024]{1,0:T(8,128)S(1)} %copy-done.3, f32[4,256]{1,0:T(4,128)S(1)} %copy-done.5, ...), custom_call_target="tpu_custom_call" | custom-call | tf_op jit(solution)/shard_map/pallas_call | solution.py:82
  268.0 53.5 %shard_map.111 = bf16[1024,512]{1,0:T(8,128)(2,1)} custom-call(bf16[1024,256]{1,0:T(8,128)(2,1)} %copy-done.1, bf16[8,256,512]{2,1,0:T(8,128)(2,1)} %bitcast.51), custom_call_target="tpu_custom_call" | custom-call | tf_op jit(solution)/shard_map/pallas_call | solution.py:260
  321.6 22.9 %reduce-scatter.2.cloned.1.call-done = bf16[256,512]{1,0:T(8,128)(2,1)} async-done(((bf16[1024,512]{1,0:T(8,128)(2,1)}), bf16[256,512]{1,0:T(8,128)(2,1)}) %reduce-scatter.2.cloned.1.call-update) | async-done | bytes 262160 | tf_op jit(solution)/shard_map/reduce_scatter | solution.py:345
  345.5 5.5 %collective-permute-start.1 = (bf16[128,512]{1,0:T(8,128)(2,1)S(1)}, bf16[128,512]{1,0:T(8,128)(2,1)S(1)}, u32[]{:S(2)}, u32[]{:S(2)}) collective-permute-start(bf16[128,512]{1,0:T(8,128)(2,1)S(1)} %get-tuple-element.14), channel_id=1, source_target_pairs={{0,0},{1,8},{2,16},{3,24},{4,4},{5,12},{6,20},{7,28},{8,1},{9,9},{... | collective-permute-start | bytes 393224 | tf_op jit(solution)/shard_map/ppermute | solution.py:357
  350.9 1.5 collective-permute-start.2
  352.4 8.7 %collective-permute-done.1 = bf16[128,512]{1,0:T(8,128)(2,1)S(1)} collective-permute-done((bf16[128,512]{1,0:T(8,128)(2,1)S(1)}, bf16[128,512]{1,0:T(8,128)(2,1)S(1)}, u32[]{:S(2)}, u32[]{:S(2)}) %collective-permute-start.1) | collective-permute-done | bytes 131104 | tf_op jit(solution)/shard_map/ppermute | solution.py:357
  361.4 3.2 collective-permute-done.2
  364.9 2.3 dynamic_update_slice.6
  367.2 2.3 dynamic_update_slice.7
  (53 shorter events, 16.7 us)
Async XLA Ops:
  6.5 154.7 %copy-start = (bf16[2048,544]{0,1:T(8,128)(2,1)S(1)}, bf16[2048,544]{0,1:T(8,128)(2,1)}, u32[]{:S(2)}) copy-start(bf16[2048,544]{0,1:T(8,128)(2,1)} %param.16) | copy-start | bytes 6684676
  6.5 19.2 %all-gather.3.cloned.1.call-start = ((), (), s32[]{:S(2)}) async-start(), calls=%async_computation.3 | async-start | bytes 1310720 | tf_op jit(solution)/shard_map/all_gather | solution.py:299
  29.9 35.0 %all-to-all-start = ((bf16[128,8,512]{2,0,1:T(8,128)(2,1)}), bf16[128,8,512]{2,0,1:T(8,128)(2,1)S(1)}, u32[]{:S(2)}, u32[]{:S(2)}) async-start(bf16[128,8,512]{2,0,1:T(8,128)(2,1)} %bitcast.49), calls=%async_computation | async-start | bytes 2097152 | tf_op jit(solution)/shard_map/all_to_all | solution.py:303
  35.7 159.2 %all-reduce.2.cloned.1.call-start = ((), (), s32[]{:S(2)}) async-start(), calls=%async_computation.4 | async-start | bytes 557056 | tf_op jit(solution)/shard_map/psum | solution.py:317
  64.9 1.0 copy-start.9
  65.9 92.8 %copy-start.11 = (f32[4,2048]{1,0:T(4,128)S(1)}, f32[4,2048]{1,0:T(4,128)}, u32[]{:S(2)}) copy-start(f32[4,2048]{1,0:T(4,128)} %param.14) | copy-start | bytes 98308
  65.9 95.4 %copy-start.12 = (f32[2048]{0:T(1024)S(1)}, f32[2048]{0:T(1024)}, u32[]{:S(2)}) copy-start(f32[2048]{0:T(1024)} %param.15) | copy-start | bytes 24580
  155.9 4.2 %collective-permute-start = (bf16[3,2048]{1,0:T(4,128)(2,1)S(1)}, bf16[3,2048]{1,0:T(4,128)(2,1)S(1)}, u32[]{:S(2)}, u32[]{:S(2)}) collective-permute-start(bf16[3,2048]{1,0:T(4,128)(2,1)S(1)} %slice.61), channel_id=1, source_target_pairs={{0,4},{4,8},{8,12},{12,16},{16,20},{20,24},{24,28},{1,5},{5,9},{9,... | collective-permute-start | bytes 36872 | tf_op jit(solution)/shard_map/ppermute | solution.py:309
  161.3 40.0 %copy-start.10 = (bf16[128,2048]{1,0:T(8,128)(2,1)S(1)}, bf16[128,2048]{1,0:T(8,128)(2,1)}, u32[]{:S(2)}) copy-start(bf16[128,2048]{1,0:T(8,128)(2,1)} %get-tuple-element.7) | copy-start | bytes 1572868
  163.2 82.6 %all-gather.5.cloned.1.call-start = ((), (), s32[]{:S(2)}) async-start(), calls=%async_computation.5 | async-start | bytes 1327104 | tf_op jit(solution)/shard_map/all_gather | solution.py:323
  202.1 49.1 %all-to-all-start.1 = ((bf16[128,8,256]{2,0,1:T(8,128)(2,1)}), bf16[128,8,256]{2,0,1:T(8,128)(2,1)}, u32[]{:S(2)}, u32[]{:S(2)}) async-start(bf16[128,8,256]{2,0,1:T(8,128)(2,1)} %bitcast.40), calls=%async_computation.1 | async-start | bytes 1048576 | tf_op jit(solution)/shard_map/all_to_all | solution.py:308
  208.0 136.4 %reduce-scatter.2.cloned.1.call-start = ((), (), s32[]{:S(2)}) async-start(), calls=%async_computation.6 | async-start | bytes 1310720 | tf_op jit(solution)/shard_map/reduce_scatter | solution.py:345
  251.2 1.0 copy-start.2
  252.2 0.8 copy-start.3
  253.1 0.8 copy-start.4
  253.9 0.7 copy-start.5
  254.6 0.7 copy-start.6
  255.2 0.6 copy-start.7
  255.9 0.6 copy-start.8
  267.2 0.8 copy-start.1
  345.5 15.7 %collective-permute-start.1 = (bf16[128,512]{1,0:T(8,128)(2,1)S(1)}, bf16[128,512]{1,0:T(8,128)(2,1)S(1)}, u32[]{:S(2)}, u32[]{:S(2)}) collective-permute-start(bf16[128,512]{1,0:T(8,128)(2,1)S(1)} %get-tuple-element.14), channel_id=1, source_target_pairs={{0,0},{1,8},{2,16},{3,24},{4,4},{5,12},{6,20},{7,28},{8,1},{9,9},{... | collective-permute-start | bytes 393224 | tf_op jit(solution)/shard_map/ppermute | solution.py:357
  350.9 13.6 %collective-permute-start.2 = (bf16[128,512]{1,0:T(8,128)(2,1)S(1)}, bf16[128,512]{1,0:T(8,128)(2,1)S(1)}, u32[]{:S(2)}, u32[]{:S(2)}) collective-permute-start(bf16[128,512]{1,0:T(8,128)(2,1)S(1)} %get-tuple-element.13), channel_id=1, source_target_pairs={{0,4},{1,12},{2,20},{3,28},{4,0},{5,8},{6,16},{7,24},{8,5},{9,13},... | collective-permute-start | bytes 393224 | tf_op jit(solution)/shard_map/ppermute | solution.py:357
Sparse Core Ops, SparseCore 0:
  8.9 16.7 all-gather.2
  163.3 31.5 all-reduce.1
  197.4 48.3 all-gather.4
  321.7 22.7 reduce-scatter.1

commit v3 on v2

--- a/solution.py
+++ b/solution.py
@@ -274,6 +274,130 @@
     )(gated, weights)
 
 
+def feature_kernel(
+    n,
+    m,
+    states,
+    activated,
+    x_proj,
+    out,
+    part,
+    got,
+    block,
+    slots,
+    sum_send,
+    sum_recv,
+    all_send,
+    all_recv,
+    ring_send,
+    ring_recv,
+):
+    place, index_at = ring_place(n)
+    targets = (index_at(place + 1), index_at(place + n - 1))
+    ch = lax.axis_index("ch")
+    peers = [lax.rem(ch + k, m) for k in range(1, m)]
+    barrier = pltpu.get_barrier_semaphore()
+    for axis, others in (("seq", targets), ("ch", peers)):
+        for other in others:
+            pl.semaphore_signal(
+                barrier, inc=1, device_id={axis: other}, device_id_type=pl.DeviceIdType.MESH
+            )
+    pl.semaphore_wait(barrier, 2 + len(peers))
+    rows = block.shape[1]
+    rank = x_proj.shape[1] - 2 * states
+
+    for k in range(m):
+        owned = pl.ds(pl.multiple_of(k * rows, rows), rows)
+        part[k] = jnp.dot(activated[owned, :], x_proj[...], preferred_element_type=jnp.float32)
+    copies = [
+        pltpu.make_async_remote_copy(
+            src_ref=part.at[peer],
+            dst_ref=got.at[k],
+            send_sem=sum_send.at[k],
+            recv_sem=sum_recv.at[k],
+            device_id={"ch": peer},
+            device_id_type=pl.DeviceIdType.MESH,
+        )
+        for k, peer in enumerate(peers)
+    ]
+    for copy in copies:
+        copy.start()
+    for copy in copies:
+        copy.wait()
+    total = part[ch]
+    for k in range(m - 1):
+        total = total + got[k]
+    tail = total[:, rank:]
+    high = tail.astype(jnp.bfloat16)
+    low = (tail - high.astype(jnp.float32)).astype(jnp.bfloat16)
+    block[ch] = jnp.concatenate([total[:, :rank].astype(jnp.bfloat16), high, low], axis=1)
+    copies = [
+        pltpu.make_async_remote_copy(
+            src_ref=block.at[ch],
+            dst_ref=block.at[ch],
+            send_sem=all_send.at[k],
+            recv_sem=all_recv.at[k],
+            device_id={"ch": peer},
+            device_id_type=pl.DeviceIdType.MESH,
+        )
+        for k, peer in enumerate(peers)
+    ]
+    for copy in copies:
+        copy.start()
+    for copy in copies:
+        copy.wait()
+
+    half = m // 2
+    for way in range(2):
+        slots[way, 0] = block[way * half : (way + 1) * half]
+
+    def keep(way, step):
+        owner = index_at(place + (n - step if way == 0 else step))
+        out[owner, way * half : (way + 1) * half] = slots[way, step]
+
+    def turn(step, _):
+        copies = [push(slots, way, step, targets[way], ring_send, ring_recv) for way in range(2)]
+        for copy in copies:
+            copy.start()
+        for way in range(2):
+            keep(way, step)
+        for copy in copies:
+            copy.wait()
+        return 0
+
+    lax.fori_loop(0, n - 1, turn, 0)
+    for way in range(2):
+        keep(way, n - 1)
+
+
+def gather_features(activated, x_proj, n, m, states):
+    rows = activated.shape[0] // m
+    inner = x_proj.shape[1]
+    wide = inner + 2 * states
+    vmem = pl.BlockSpec(memory_space=pltpu.VMEM)
+    return pl.pallas_call(
+        functools.partial(feature_kernel, n, m, states),
+        out_shape=jax.ShapeDtypeStruct((n, m, rows, wide), jnp.bfloat16),
+        in_specs=[vmem] * 2,
+        out_specs=vmem,
+        scratch_shapes=[
+            pltpu.VMEM((m, rows, inner), jnp.float32),
+            pltpu.VMEM((m - 1, rows, inner), jnp.float32),
+            pltpu.VMEM((m, rows, wide), jnp.bfloat16),
+            pltpu.VMEM((2, n, m // 2, rows, wide), jnp.bfloat16),
+            pltpu.SemaphoreType.DMA((m - 1,)),
+            pltpu.SemaphoreType.DMA((m - 1,)),
+            pltpu.SemaphoreType.DMA((m - 1,)),
+            pltpu.SemaphoreType.DMA((m - 1,)),
+            pltpu.SemaphoreType.DMA((2, n - 1)),
+            pltpu.SemaphoreType.DMA((2, n - 1)),
+        ],
+        compiler_params=pltpu.CompilerParams(
+            collective_id=2, has_side_effects=True, vmem_limit_bytes=40 * 1024 * 1024
+        ),
+    )(activated, x_proj)
+
+
 def on_device(
     tokens,
     norm_gain,
@@ -297,13 +421,15 @@
     states = a_log.shape[1]
 
     token_rows = lax.all_gather(tokens, "ch", axis=1, tiled=True)
+    w_conv = in_proj[:, 0, :]
+    w_gate = in_proj[:, 1, :].reshape(-1, n_seq, width).transpose(1, 0, 2)
+    token_rows, w_conv, w_gate = lax.optimization_barrier((token_rows, w_conv, w_gate))
     tokens_wide = token_rows.astype(jnp.float32)
     scale_rows = lax.rsqrt(jnp.mean(tokens_wide * tokens_wide, axis=-1, keepdims=True) + 1e-06)
     normed = (tokens_wide * scale_rows * norm_gain).astype(jnp.bfloat16)
     columns = lax.all_to_all(normed, "seq", split_axis=1, concat_axis=0, tiled=True)
 
-    w_gate = in_proj[:, 1, :].reshape(-1, n_seq, width).transpose(1, 0, 2)
-    conv_tokens, gate = project(columns, in_proj[:, 0, :], w_gate)
+    conv_tokens, gate = project(columns, w_conv, w_gate)
 
     conv_columns = lax.all_to_all(conv_tokens, "seq", split_axis=1, concat_axis=0, tiled=True)
     earlier = lax.ppermute(
@@ -314,13 +440,8 @@
     for tap in range(TAPS):
         convolved = convolved + conv_weight[tap] * padded[tap : tap + local_tokens]
     activated_half = jax.nn.silu(convolved).astype(jnp.bfloat16)
-    features = lax.psum(
-        jnp.dot(activated_half, x_proj, preferred_element_type=jnp.float32), "ch"
-    )
-    tail = features[:, rank:]
-    high = lax.reduce_precision(tail, 8, 7)
-    sent = jnp.concatenate([features[:, :rank], high, tail - high], 1).astype(jnp.bfloat16)
-    everyone = lax.all_gather(sent, "seq", axis=0, tiled=True)
+    everyone = gather_features(activated_half, x_proj, n_seq, n_ch, states)
+    everyone = everyone.reshape(all_tokens, -1)
     step_raw = everyone[:, :rank]
     pair = everyone[:, rank:].astype(jnp.float32)
     bc_rows = (pair[:, : 2 * states] + pair[:, 2 * states :]).T

time: 378 us -> 343 us (0.907)
  waiting for transfers between devices: 123 us -> 61.2 us
  Pallas kernels: 153 us -> 187 us
    pallas_call x0 -> x1, Pallas kernels: none -> 39.1 us  [gather_features(): pl.pallas_call(functools.partial(feature_kernel, n, m, states), out_shape...]
    all_gather x1 -> x0, waiting for transfers between devices: 36.2 us -> none  [on_device(): everyone = lax.all_gather(sent, 'seq', axis=0, tiled=True)]
    psum x1 -> x0, waiting for transfers between devices: 31.6 us -> none  [on_device(): lax.psum(jnp.dot(activated_half, x_proj, preferred_element_type=jnp.float...]
    all_to_all x1, waiting for transfers between devices: 0.01 us -> 24.9 us  [on_device(): lax.all_to_all(normed, 'seq', split_axis=1, concat_axis=0, tiled=True)]
    all_gather x1, waiting for transfers between devices: 18.5 us -> 0.01 us  [on_device(): token_rows = lax.all_gather(tokens, 'ch', axis=1, tiled=True)]
    unnamed x29 -> x31, local copies, waits for them, and re-layouts: 23.2 us -> 28.1 us
    pallas_call x1, Pallas kernels: 53.5 us -> 49.3 us  [gather_project(): pl.pallas_call(functools.partial(gather_kernel, n), out_shape=jax.ShapeDt...]
  transfers between devices with their start and end apart: 9 -> 7, of which waited for: 7 -> 4; matrix products, arithmetic and copies ran while one was open for 11% -> 12% of each run, Pallas kernels for 0% -> 11%
where the time goes in v3:
time: 343 us; the launch traced here: 342 us
  Pallas kernels  187 us (55%)
  waiting for transfers between devices  61.2 us (18%)
  local copies, waits for them, and re-layouts  56.3 us (16%)
  starting transfers between devices  19.9 us (6%)
  between operations  13.7 us (4%)
  other arithmetic  3.93 us (1%)
    pallas_call x1, Pallas kernels, project(): pl.pallas_call(functools.partial(project_kernel, n), out_shape=(jax.Shape...  87.9 us
    pallas_call x1, Pallas kernels, gather_project(): pl.pallas_call(functools.partial(gather_kernel, n), out_shape=jax.ShapeDt...  49.3 us
    pallas_call x1, Pallas kernels, gather_features(): pl.pallas_call(functools.partial(feature_kernel, n, m, states), out_shape...  39.1 us
    unnamed x31, local copies, waits for them, and re-layouts  28.1 us
    all_to_all x1, waiting for transfers between devices, on_device(): lax.all_to_all(normed, 'seq', split_axis=1, concat_axis=0, tiled=True)  24.9 us
    reduce_scatter x1, waiting for transfers between devices, on_device(): lax.psum_scatter(partial_out, 'ch', scatter_dimension=0, tiled=True)  23.6 us
    ppermute x2, waiting for transfers between devices, on_device(): arrived = lax.ppermute(block, ('seq', 'ch'), route)  11.9 us
    pallas_call x1, Pallas kernels, run_scan(): pl.pallas_call(scan_kernel, out_shape=jax.ShapeDtypeStruct((tokens, width...  10.7 us
  transfers between devices with their start and end apart: 7, of which 4 were waited for; matrix products, arithmetic and copies ran while one was open for 12% of the time, Pallas kernels for 11%

profile of v3, /device:TPU:2, one launch (start us, length us, event | category | flops | bytes accessed | tf_op | source)
XLA Modules:
  0.0 342.0 jit_solution(13407385122255448573)
XLA Ops:
  7.3 9.9 %fusion.8 = (bf16[512,1,2048]{2,1,0:T(2,128)(2,1)}, bf16[512,1,2048]{2,1,0:T(2,128)(2,1)}) fusion(bf16[512,2,2048]{2,1,0:T(2,128)(2,1)} %param.13), kind=kLoop, calls=%fused_computation.26 | loop fusion | bytes 8388608 | tf_op jit(solution)/shard_map/slice | solution.py:425
  17.2 10.5 %copy.28 = bf16[512,1,2048]{0,2,1:T(8,128)(2,1)} copy(bf16[512,1,2048]{2,1,0:T(2,128)(2,1)} %get-tuple-element.15) | data formatting | bytes 4194304
  27.7 3.9 %copy.20 = bf16[512,8,256]{2,0,1:T(8,128)(2,1)} copy(bf16[512,8,256]{0,2,1:T(8,128)(2,1)} %bitcast.47) | data formatting | bytes 4194304 | tf_op jit(solution)/shard_map/reshape;squeeze | solution.py:425
  31.6 4.9 %copy.36 = bf16[512,1,2048]{2,0,1:T(8,128)(2,1)} copy(bf16[512,1,2048]{2,1,0:T(2,128)(2,1)} %get-tuple-element.16) | data formatting | bytes 4194304
  36.5 1.5 fusion
  38.0 1.5 fusion.2
  39.6 1.1 copy.37
  40.6 5.9 %all-to-all-start = ((bf16[128,8,512]{2,0,1:T(8,128)(2,1)}), bf16[128,8,512]{2,0,1:T(8,128)(2,1)S(1)}, u32[]{:S(2)}, u32[]{:S(2)}) async-start(bf16[128,8,512]{2,0,1:T(8,128)(2,1)} %bitcast.51), calls=%async_computation | async-start | bytes 2097152 | tf_op jit(solution)/shard_map/all_to_all | solution.py:430
  47.4 24.9 %all-to-all-done = bf16[128,8,512]{2,0,1:T(8,128)(2,1)S(1)} async-done(((bf16[128,8,512]{2,0,1:T(8,128)(2,1)}), bf16[128,8,512]{2,0,1:T(8,128)(2,1)S(1)}, u32[]{:S(2)}, u32[]{:S(2)}) %all-to-all-start) | async-done | bytes 1048608 | tf_op jit(solution)/shard_map/all_to_all | solution.py:430
  72.3 1.0 copy-done.8
  73.3 87.9 %shard_map.109 = (bf16[128,2048]{1,0:T(8,128)(2,1)}, bf16[1024,256]{1,0:T(8,128)(2,1)}) custom-call(bf16[1024,512]{1,0:T(8,128)(2,1)} %bitcast.49, bf16[512,2048]{1,0:T(8,128)(2,1)} %bitcast.46, bf16[8,512,256]{2,1,0:T(8,128)(2,1)} %bitcast.48), custom_call_target="tpu_custom_call" | custom-call | tf_op jit(solution)/shard_map/pallas_call | solution.py:203
  162.0 2.8 collective-permute-start
  165.5 4.4 %copy.23.x_proj = bf16[2048,544]{1,0:T(8,128)(2,1)} copy(bf16[2048,544]{0,1:T(8,128)(2,1)} %param.16) | data formatting | bytes 4456448 | tf_op args[5]
  170.5 1.3 dynamic_slice.28
  171.8 1.3 dynamic_slice.30
  173.2 0.8 copy.38
  174.0 4.1 %all-to-all-start.1 = ((bf16[128,8,256]{2,0,1:T(8,128)(2,1)}), bf16[128,8,256]{2,0,1:T(8,128)(2,1)}, u32[]{:S(2)}, u32[]{:S(2)}) async-start(bf16[128,8,256]{2,0,1:T(8,128)(2,1)} %bitcast.40), calls=%async_computation.1 | async-start | bytes 1048576 | tf_op jit(solution)/shard_map/all_to_all | solution.py:434
  179.0 1.0 copy-done.1
  180.1 39.1 %shard_map.110 = bf16[8,4,32,576]{3,2,1,0:T(8,128)(2,1)S(1)} custom-call(bf16[128,2048]{1,0:T(8,128)(2,1)S(1)} %multiply_convert_fusion.activated, bf16[2048,544]{1,0:T(8,128)(2,1)S(1)} %copy-done.1), custom_call_target="tpu_custom_call" | custom-call | tf_op jit(solution)/shard_map/pallas_call | solution.py:378
  220.0 1.1 copy.29
  221.2 1.0 copy-done.3
  224.9 10.7 %shard_map.111.gated = bf16[1024,256]{1,0:T(8,128)(2,1)S(1)} custom-call(bf16[1024,256]{1,0:T(8,128)(2,1)} %bitcast.6.conv_input, bf16[1024,256]{1,0:T(8,128)(2,1)S(1)} %copy-done.3, bf16[1024,512]{1,0:T(8,128)(2,1)S(1)} %slice.72.step_raw, f32[16,1024]{1,0:T(8,128)S(1)} %get-tuple-element.20.b_rows, f32[16,1024]{1,0:T(8,128)S(1)} %get-tuple-element.19.c_rows, ...), custom_call_target="tpu_custom_call" | custom-call | tf_op jit(solution)/shard_map/pallas_call | solution.py:82
  235.6 0.8 copy-done.2
  236.4 49.3 %shard_map.112 = bf16[1024,512]{1,0:T(8,128)(2,1)} custom-call(bf16[1024,256]{1,0:T(8,128)(2,1)} %copy-done.2, bf16[8,256,512]{2,1,0:T(8,128)(2,1)} %bitcast.53), custom_call_target="tpu_custom_call" | custom-call | tf_op jit(solution)/shard_map/pallas_call | solution.py:260
  285.8 23.6 %reduce-scatter.2.cloned.1.call-done = bf16[256,512]{1,0:T(8,128)(2,1)} async-done(((bf16[1024,512]{1,0:T(8,128)(2,1)}), bf16[256,512]{1,0:T(8,128)(2,1)}) %reduce-scatter.2.cloned.1.call-update) | async-done | bytes 262160 | tf_op jit(solution)/shard_map/reduce_scatter | solution.py:466
  309.4 1.0 dynamic-slice_bitcast_fusion
  310.4 5.5 %collective-permute-start.1 = (bf16[128,512]{1,0:T(8,128)(2,1)S(1)}, bf16[128,512]{1,0:T(8,128)(2,1)S(1)}, u32[]{:S(2)}, u32[]{:S(2)}) collective-permute-start(bf16[128,512]{1,0:T(8,128)(2,1)S(1)} %get-tuple-element.18), channel_id=1, source_target_pairs={{0,0},{1,8},{2,16},{3,24},{4,4},{5,12},{6,20},{7,28},{8,1},{9,9},{... | collective-permute-start | bytes 393224 | tf_op jit(solution)/shard_map/ppermute | solution.py:478
  315.8 1.5 collective-permute-start.2
  317.3 8.7 %collective-permute-done.1 = bf16[128,512]{1,0:T(8,128)(2,1)S(1)} collective-permute-done((bf16[128,512]{1,0:T(8,128)(2,1)S(1)}, bf16[128,512]{1,0:T(8,128)(2,1)S(1)}, u32[]{:S(2)}, u32[]{:S(2)}) %collective-permute-start.1) | collective-permute-done | bytes 131104 | tf_op jit(solution)/shard_map/ppermute | solution.py:478
  326.2 3.2 collective-permute-done.2
  329.8 2.3 dynamic_update_slice.6
  332.1 2.3 dynamic_update_slice.7
  (47 shorter events, 9.2 us)
Async XLA Ops:
  6.5 40.8 %copy-start = (bf16[512,2048]{1,0:T(8,128)(2,1)S(1)}, bf16[512,2048]{1,0:T(8,128)(2,1)}, u32[]{:S(2)}) copy-start(bf16[512,2048]{1,0:T(8,128)(2,1)} %param.17) | copy-start | bytes 6291460
  6.5 29.9 %all-gather.2.cloned.1.call-start = ((), (), s32[]{:S(2)}) async-start(), calls=%async_computation.3 | async-start | bytes 1310720 | tf_op jit(solution)/shard_map/all_gather | solution.py:423
  31.6 6.4 %copy-start.11 = (f32[4096]{0:T(1024)S(1)}, f32[4096]{0:T(1024)}, u32[]{:S(2)}) copy-start(f32[4096]{0:T(1024)} %param.12) | copy-start | bytes 49156
  39.5 7.8 %copy-start.10 = (f32[4,2048]{1,0:T(4,128)S(1)}, f32[4,2048]{1,0:T(4,128)}, u32[]{:S(2)}) copy-start(f32[4,2048]{1,0:T(4,128)} %param.14) | copy-start | bytes 98308
  40.6 31.6 %all-to-all-start = ((bf16[128,8,512]{2,0,1:T(8,128)(2,1)}), bf16[128,8,512]{2,0,1:T(8,128)(2,1)S(1)}, u32[]{:S(2)}, u32[]{:S(2)}) async-start(bf16[128,8,512]{2,0,1:T(8,128)(2,1)} %bitcast.51), calls=%async_computation | async-start | bytes 2097152 | tf_op jit(solution)/shard_map/all_to_all | solution.py:430
  72.3 1.0 copy-start.8
  162.0 16.2 %collective-permute-start = (bf16[3,2048]{1,0:T(4,128)(2,1)S(1)}, bf16[3,2048]{1,0:T(4,128)(2,1)S(1)}, u32[]{:S(2)}, u32[]{:S(2)}) collective-permute-start(bf16[3,2048]{1,0:T(4,128)(2,1)S(1)} %slice.54), channel_id=1, source_target_pairs={{0,4},{4,8},{8,12},{12,16},{16,20},{20,24},{24,28},{1,5},{5,9},{9,... | collective-permute-start | bytes 36872 | tf_op jit(solution)/shard_map/ppermute | solution.py:435
  165.5 4.4 %copy-start.12 = (f32[2048]{0:T(1024)S(1)}, f32[2048]{0:T(1024)}, u32[]{:S(2)}) copy-start(f32[2048]{0:T(1024)} %param.15) | copy-start | bytes 24580
  165.5 7.7 %copy-start.9 = (bf16[128,2048]{1,0:T(8,128)(2,1)S(1)}, bf16[128,2048]{1,0:T(8,128)(2,1)}, u32[]{:S(2)}) copy-start(bf16[128,2048]{1,0:T(8,128)(2,1)} %get-tuple-element.13) | copy-start | bytes 1572868
  174.0 47.2 %all-to-all-start.1 = ((bf16[128,8,256]{2,0,1:T(8,128)(2,1)}), bf16[128,8,256]{2,0,1:T(8,128)(2,1)}, u32[]{:S(2)}, u32[]{:S(2)}) async-start(bf16[128,8,256]{2,0,1:T(8,128)(2,1)} %bitcast.40), calls=%async_computation.1 | async-start | bytes 1048576 | tf_op jit(solution)/shard_map/all_to_all | solution.py:434
  178.1 131.2 %reduce-scatter.2.cloned.1.call-start = ((), (), s32[]{:S(2)}) async-start(), calls=%async_computation.4 | async-start | bytes 1310720 | tf_op jit(solution)/shard_map/reduce_scatter | solution.py:466
  178.3 1.7 copy-start.1
  221.2 1.0 copy-start.3
  222.2 0.7 copy-start.4
  222.9 0.7 copy-start.5
  223.5 0.7 copy-start.6
  224.2 0.7 copy-start.7
  235.6 0.8 copy-start.2
  310.4 15.7 %collective-permute-start.1 = (bf16[128,512]{1,0:T(8,128)(2,1)S(1)}, bf16[128,512]{1,0:T(8,128)(2,1)S(1)}, u32[]{:S(2)}, u32[]{:S(2)}) collective-permute-start(bf16[128,512]{1,0:T(8,128)(2,1)S(1)} %get-tuple-element.18), channel_id=1, source_target_pairs={{0,0},{1,8},{2,16},{3,24},{4,4},{5,12},{6,20},{7,28},{8,1},{9,9},{... | collective-permute-start | bytes 393224 | tf_op jit(solution)/shard_map/ppermute | solution.py:478
  315.8 13.6 %collective-permute-start.2 = (bf16[128,512]{1,0:T(8,128)(2,1)S(1)}, bf16[128,512]{1,0:T(8,128)(2,1)S(1)}, u32[]{:S(2)}, u32[]{:S(2)}) collective-permute-start(bf16[128,512]{1,0:T(8,128)(2,1)S(1)} %get-tuple-element.17), channel_id=1, source_target_pairs={{0,4},{1,12},{2,20},{3,28},{4,0},{5,8},{6,16},{7,24},{8,5},{9,13},... | collective-permute-start | bytes 393224 | tf_op jit(solution)/shard_map/ppermute | solution.py:478
Sparse Core Ops, SparseCore 0:
  8.9 16.7 all-gather.1
  285.8 23.4 reduce-scatter.1

commit v4 on v3

--- a/solution.py
+++ b/solution.py
@@ -221,11 +221,21 @@
     )(columns, w_conv, w_gate)
 
 
-def gather_kernel(n, gated, weights, out, slots, totals, send_sem, recv_sem):
+def gather_kernel(
+    n, m, gated, weights, out, slots, totals, parts, got, send_sem, recv_sem, sum_send, sum_recv
+):
     place, index_at = ring_place(n)
     targets = (index_at(place + 1), index_at(place + n - 1))
     rows_half = slots.shape[2]
-    greet(targets)
+    ch = lax.axis_index("ch")
+    peers = [lax.rem(ch + k, m) for k in range(1, m)]
+    barrier = pltpu.get_barrier_semaphore()
+    for axis, others in (("seq", targets), ("ch", peers)):
+        for other in others:
+            pl.semaphore_signal(
+                barrier, inc=1, device_id={axis: other}, device_id_type=pl.DeviceIdType.MESH
+            )
+    pl.semaphore_wait(barrier, 2 + len(peers))
 
     def add(way, step):
         owner = index_at(place + (n - step if way == 0 else step))
@@ -250,23 +260,50 @@
     lax.fori_loop(0, n - 1, turn, 0)
     for way in range(2):
         add(way, n - 1)
-        out[way * rows_half : (way + 1) * rows_half, :] = totals[way].astype(out.dtype)
-
-
-def gather_project(gated, weights):
+    rows = out.shape[0]
+    half = m // 2
+    for k in range(m):
+        start = (k % half) * rows
+        parts[k] = totals[k // half, start : start + rows, :].astype(parts.dtype)
+    copies = [
+        pltpu.make_async_remote_copy(
+            src_ref=parts.at[peer],
+            dst_ref=got.at[k],
+            send_sem=sum_send.at[k],
+            recv_sem=sum_recv.at[k],
+            device_id={"ch": peer},
+            device_id_type=pl.DeviceIdType.MESH,
+        )
+        for k, peer in enumerate(peers)
+    ]
+    for copy in copies:
+        copy.start()
+    for copy in copies:
+        copy.wait()
+    summed = parts[ch].astype(jnp.float32)
+    for k in range(m - 1):
+        summed = summed + got[k].astype(jnp.float32)
+    out[...] = summed.astype(out.dtype)
+
+
+def gather_project(gated, weights, m):
     n, width, out_width = weights.shape
     total = gated.shape[0]
     vmem = pl.BlockSpec(memory_space=pltpu.VMEM)
     return pl.pallas_call(
-        functools.partial(gather_kernel, n),
-        out_shape=jax.ShapeDtypeStruct((total, out_width), jnp.bfloat16),
+        functools.partial(gather_kernel, n, m),
+        out_shape=jax.ShapeDtypeStruct((total // m, out_width), jnp.bfloat16),
         in_specs=[vmem] * 2,
         out_specs=vmem,
         scratch_shapes=[
             pltpu.VMEM((2, n, total // 2, width), jnp.bfloat16),
             pltpu.VMEM((2, total // 2, out_width), jnp.float32),
+            pltpu.VMEM((m, total // m, out_width), jnp.bfloat16),
+            pltpu.VMEM((m - 1, total // m, out_width), jnp.bfloat16),
             pltpu.SemaphoreType.DMA((2, n - 1)),
             pltpu.SemaphoreType.DMA((2, n - 1)),
+            pltpu.SemaphoreType.DMA((m - 1,)),
+            pltpu.SemaphoreType.DMA((m - 1,)),
         ],
         compiler_params=pltpu.CompilerParams(
             collective_id=1, has_side_effects=True, vmem_limit_bytes=56 * 1024 * 1024
@@ -423,7 +460,7 @@
     token_rows = lax.all_gather(tokens, "ch", axis=1, tiled=True)
     w_conv = in_proj[:, 0, :]
     w_gate = in_proj[:, 1, :].reshape(-1, n_seq, width).transpose(1, 0, 2)
-    token_rows, w_conv, w_gate = lax.optimization_barrier((token_rows, w_conv, w_gate))
+    token_rows, w_conv = lax.optimization_barrier((token_rows, w_conv))
     tokens_wide = token_rows.astype(jnp.float32)
     scale_rows = lax.rsqrt(jnp.mean(tokens_wide * tokens_wide, axis=-1, keepdims=True) + 1e-06)
     normed = (tokens_wide * scale_rows * norm_gain).astype(jnp.bfloat16)
@@ -462,8 +499,7 @@
         mine(a_log, 0).T,
         mine(d_skip, 0)[None],
     )
-    partial_out = gather_project(gated, out_proj.reshape(n_seq, width, -1))
-    summed = lax.psum_scatter(partial_out, "ch", scatter_dimension=0, tiled=True)
+    summed = gather_project(gated, out_proj.reshape(n_seq, width, -1), n_ch)
     share = n_seq // n_ch
     out_width = out_proj.shape[1]
     blocks = summed.reshape(share, local_tokens, out_width)

time: 343 us -> 317 us (0.924)
  waiting for transfers between devices: 61.2 us -> 29.2 us
  Pallas kernels: 187 us -> 196 us
    reduce_scatter x1 -> x0, waiting for transfers between devices: 23.6 us -> none  [on_device(): lax.psum_scatter(partial_out, 'ch', scatter_dimension=0, tiled=True)]
    all_to_all x1, waiting for transfers between devices: 24.9 us -> 10.9 us  [on_device(): lax.all_to_all(normed, 'seq', split_axis=1, concat_axis=0, tiled=True)]
    pallas_call x1, Pallas kernels: 49.3 us -> 58.1 us  [gather_project(): pl.pallas_call(functools.partial(gather_kernel, n, m), out_shape=jax.Shap...]
    all_gather x1, waiting for transfers between devices: 0.01 us -> 6.29 us  [on_device(): token_rows = lax.all_gather(tokens, 'ch', axis=1, tiled=True)]
  transfers between devices with their start and end apart: 7 -> 6, of which waited for: 4 -> 4; matrix products, arithmetic and copies ran while one was open for 12% -> 12% of each run, Pallas kernels for 11% -> 12%
where the time goes in v4:
time: 317 us; the launch traced here: 316 us
  Pallas kernels  196 us (62%)
  local copies, waits for them, and re-layouts  53.8 us (17%)
  waiting for transfers between devices  29.2 us (9%)
  starting transfers between devices  19.2 us (6%)
  between operations  13.6 us (4%)
  other arithmetic  3.93 us (1%)
    pallas_call x1, Pallas kernels, project(): pl.pallas_call(functools.partial(project_kernel, n), out_shape=(jax.Shape...  88 us
    pallas_call x1, Pallas kernels, gather_project(): pl.pallas_call(functools.partial(gather_kernel, n, m), out_shape=jax.Shap...  58.1 us
    pallas_call x1, Pallas kernels, gather_features(): pl.pallas_call(functools.partial(feature_kernel, n, m, states), out_shape...  39.4 us
    unnamed x31, local copies, waits for them, and re-layouts  25.9 us
    ppermute x2, waiting for transfers between devices, on_device(): arrived = lax.ppermute(block, ('seq', 'ch'), route)  11.3 us
    all_to_all x1, waiting for transfers between devices, on_device(): lax.all_to_all(normed, 'seq', split_axis=1, concat_axis=0, tiled=True)  10.9 us
    pallas_call x1, Pallas kernels, run_scan(): pl.pallas_call(scan_kernel, out_shape=jax.ShapeDtypeStruct((tokens, width...  10.7 us
    slice x1, local copies, waits for them, and re-layouts, on_device(): w_gate = in_proj[:, 1, :].reshape(-1, n_seq, width).transpose(1, 0, 2)  9.58 us
  transfers between devices with their start and end apart: 6, of which 4 were waited for; matrix products, arithmetic and copies ran while one was open for 12% of the time, Pallas kernels for 12%

profile of v4, /device:TPU:2, one launch (start us, length us, event | category | flops | bytes accessed | tf_op | source)
XLA Modules:
  0.0 315.9 jit_solution(16275017754249323753)
XLA Ops:
  7.3 9.6 %fusion.8 = (bf16[512,1,2048]{2,1,0:T(2,128)(2,1)}, bf16[512,1,2048]{2,1,0:T(2,128)(2,1)S(1)}) fusion(bf16[512,2,2048]{2,1,0:T(2,128)(2,1)} %param.13), kind=kLoop, calls=%fused_computation.26 | loop fusion | bytes 8388608 | tf_op jit(solution)/shard_map/slice | solution.py:462
  16.8 2.6 copy.36
  19.5 6.3 %all-gather.2.cloned.1.call-done = bf16[128,4096]{1,0:T(8,128)(2,1)} async-done(((bf16[128,1024]{1,0:T(8,128)(2,1)}), bf16[128,4096]{1,0:T(8,128)(2,1)}) %all-gather.2.cloned.1.call-update) | async-done | bytes 1048592 | tf_op jit(solution)/shard_map/all_gather | solution.py:460
  25.8 1.5 fusion
  27.3 1.5 fusion.2
  28.8 1.2 copy.37
  30.0 5.8 %all-to-all-start = ((bf16[128,8,512]{2,0,1:T(8,128)(2,1)}), bf16[128,8,512]{2,0,1:T(8,128)(2,1)S(1)}, u32[]{:S(2)}, u32[]{:S(2)}) async-start(bf16[128,8,512]{2,0,1:T(8,128)(2,1)} %bitcast.51), calls=%async_computation | async-start | bytes 2097152 | tf_op jit(solution)/shard_map/all_to_all | solution.py:467
  35.8 10.5 %copy.28 = bf16[512,1,2048]{0,2,1:T(8,128)(2,1)} copy(bf16[512,1,2048]{2,1,0:T(2,128)(2,1)} %get-tuple-element.13) | data formatting | bytes 4194304
  46.3 3.9 %copy.21 = bf16[512,8,256]{2,0,1:T(8,128)(2,1)} copy(bf16[512,8,256]{0,2,1:T(8,128)(2,1)} %bitcast.47) | data formatting | bytes 4194304 | tf_op jit(solution)/shard_map/reshape;squeeze | solution.py:462
  51.0 10.9 %all-to-all-done = bf16[128,8,512]{2,0,1:T(8,128)(2,1)S(1)} async-done(((bf16[128,8,512]{2,0,1:T(8,128)(2,1)}), bf16[128,8,512]{2,0,1:T(8,128)(2,1)S(1)}, u32[]{:S(2)}, u32[]{:S(2)}) %all-to-all-start) | async-done | bytes 1048608 | tf_op jit(solution)/shard_map/all_to_all | solution.py:467
  61.9 1.0 copy-done.8
  62.9 88.0 %shard_map.109 = (bf16[128,2048]{1,0:T(8,128)(2,1)}, bf16[1024,256]{1,0:T(8,128)(2,1)}) custom-call(bf16[1024,512]{1,0:T(8,128)(2,1)} %bitcast.49, bf16[512,2048]{1,0:T(8,128)(2,1)} %bitcast.46, bf16[8,512,256]{2,1,0:T(8,128)(2,1)} %bitcast.48), custom_call_target="tpu_custom_call" | custom-call | tf_op jit(solution)/shard_map/pallas_call | solution.py:203
  151.7 2.8 collective-permute-start
  155.2 4.4 %copy.23.x_proj = bf16[2048,544]{1,0:T(8,128)(2,1)} copy(bf16[2048,544]{0,1:T(8,128)(2,1)} %param.16) | data formatting | bytes 4456448 | tf_op args[5]
  160.2 1.3 dynamic_slice.28
  161.5 1.3 dynamic_slice.30
  162.9 0.8 copy.38
  163.7 4.1 %all-to-all-start.1 = ((bf16[128,8,256]{2,0,1:T(8,128)(2,1)}), bf16[128,8,256]{2,0,1:T(8,128)(2,1)}, u32[]{:S(2)}, u32[]{:S(2)}) async-start(bf16[128,8,256]{2,0,1:T(8,128)(2,1)} %bitcast.40), calls=%async_computation.1 | async-start | bytes 1048576 | tf_op jit(solution)/shard_map/all_to_all | solution.py:471
  168.7 1.0 copy-done.1
  169.7 39.4 %shard_map.110 = bf16[8,4,32,576]{3,2,1,0:T(8,128)(2,1)S(1)} custom-call(bf16[128,2048]{1,0:T(8,128)(2,1)S(1)} %multiply_convert_fusion.activated, bf16[2048,544]{1,0:T(8,128)(2,1)S(1)} %copy-done.1), custom_call_target="tpu_custom_call" | custom-call | tf_op jit(solution)/shard_map/pallas_call | solution.py:415
  209.9 1.1 copy.29
  211.1 1.0 copy-done.3
  214.8 10.7 %shard_map.111.gated = bf16[1024,256]{1,0:T(8,128)(2,1)S(1)} custom-call(bf16[1024,256]{1,0:T(8,128)(2,1)} %bitcast.6.conv_input, bf16[1024,256]{1,0:T(8,128)(2,1)S(1)} %copy-done.3, bf16[1024,512]{1,0:T(8,128)(2,1)S(1)} %slice.72.step_raw, f32[16,1024]{1,0:T(8,128)S(1)} %get-tuple-element.18.b_rows, f32[16,1024]{1,0:T(8,128)S(1)} %get-tuple-element.17.c_rows, ...), custom_call_target="tpu_custom_call" | custom-call | tf_op jit(solution)/shard_map/pallas_call | solution.py:82
  225.5 0.8 copy-done.2
  226.3 58.1 %shard_map.112 = bf16[256,512]{1,0:T(8,128)(2,1)} custom-call(bf16[1024,256]{1,0:T(8,128)(2,1)} %copy-done.2, bf16[8,256,512]{2,1,0:T(8,128)(2,1)} %bitcast.53), custom_call_target="tpu_custom_call" | custom-call | tf_op jit(solution)/shard_map/pallas_call | solution.py:293
  284.5 1.0 dynamic-slice_bitcast_fusion
  285.5 3.8 %collective-permute-start.1 = (bf16[128,512]{1,0:T(8,128)(2,1)S(1)}, bf16[128,512]{1,0:T(8,128)(2,1)S(1)}, u32[]{:S(2)}, u32[]{:S(2)}) collective-permute-start(bf16[128,512]{1,0:T(8,128)(2,1)S(1)} %get-tuple-element.16), channel_id=1, source_target_pairs={{0,0},{1,8},{2,16},{3,24},{4,4},{5,12},{6,20},{7,28},{8,1},{9,9},{... | collective-permute-start | bytes 393224 | tf_op jit(solution)/shard_map/ppermute | solution.py:514
  289.3 2.6 collective-permute-start.2
  291.9 9.2 %collective-permute-done.1 = bf16[128,512]{1,0:T(8,128)(2,1)S(1)} collective-permute-done((bf16[128,512]{1,0:T(8,128)(2,1)S(1)}, bf16[128,512]{1,0:T(8,128)(2,1)S(1)}, u32[]{:S(2)}, u32[]{:S(2)}) %collective-permute-start.1) | collective-permute-done | bytes 131104 | tf_op jit(solution)/shard_map/ppermute | solution.py:514
  301.4 2.0 collective-permute-done.2
  303.8 2.3 dynamic_update_slice.6
  306.1 2.3 dynamic_update_slice.7
  (44 shorter events, 9.2 us)
Async XLA Ops:
  6.5 44.4 %copy-start = (bf16[512,2048]{1,0:T(8,128)(2,1)S(1)}, bf16[512,2048]{1,0:T(8,128)(2,1)}, u32[]{:S(2)}) copy-start(bf16[512,2048]{1,0:T(8,128)(2,1)} %param.17) | copy-start | bytes 6291460
  6.5 19.2 %all-gather.2.cloned.1.call-start = ((), (), s32[]{:S(2)}) async-start(), calls=%async_computation.2 | async-start | bytes 1310720 | tf_op jit(solution)/shard_map/all_gather | solution.py:460
  16.8 10.4 %copy-start.11 = (f32[4096]{0:T(1024)S(1)}, f32[4096]{0:T(1024)}, u32[]{:S(2)}) copy-start(f32[4096]{0:T(1024)} %param.12) | copy-start | bytes 49156
  30.0 31.9 %all-to-all-start = ((bf16[128,8,512]{2,0,1:T(8,128)(2,1)}), bf16[128,8,512]{2,0,1:T(8,128)(2,1)S(1)}, u32[]{:S(2)}, u32[]{:S(2)}) async-start(bf16[128,8,512]{2,0,1:T(8,128)(2,1)} %bitcast.51), calls=%async_computation | async-start | bytes 2097152 | tf_op jit(solution)/shard_map/all_to_all | solution.py:467
  46.3 4.7 %copy-start.10 = (f32[4,2048]{1,0:T(4,128)S(1)}, f32[4,2048]{1,0:T(4,128)}, u32[]{:S(2)}) copy-start(f32[4,2048]{1,0:T(4,128)} %param.14) | copy-start | bytes 98308
  61.9 1.0 copy-start.8
  151.7 16.1 %collective-permute-start = (bf16[3,2048]{1,0:T(4,128)(2,1)S(1)}, bf16[3,2048]{1,0:T(4,128)(2,1)S(1)}, u32[]{:S(2)}, u32[]{:S(2)}) collective-permute-start(bf16[3,2048]{1,0:T(4,128)(2,1)S(1)} %slice.54), channel_id=1, source_target_pairs={{0,4},{4,8},{8,12},{12,16},{16,20},{20,24},{24,28},{1,5},{5,9},{9,... | collective-permute-start | bytes 36872 | tf_op jit(solution)/shard_map/ppermute | solution.py:472
  155.2 4.4 %copy-start.12 = (f32[2048]{0:T(1024)S(1)}, f32[2048]{0:T(1024)}, u32[]{:S(2)}) copy-start(f32[2048]{0:T(1024)} %param.15) | copy-start | bytes 24580
  155.2 7.7 %copy-start.9 = (bf16[128,2048]{1,0:T(8,128)(2,1)S(1)}, bf16[128,2048]{1,0:T(8,128)(2,1)}, u32[]{:S(2)}) copy-start(bf16[128,2048]{1,0:T(8,128)(2,1)} %get-tuple-element.11) | copy-start | bytes 1572868
  163.7 47.4 %all-to-all-start.1 = ((bf16[128,8,256]{2,0,1:T(8,128)(2,1)}), bf16[128,8,256]{2,0,1:T(8,128)(2,1)}, u32[]{:S(2)}, u32[]{:S(2)}) async-start(bf16[128,8,256]{2,0,1:T(8,128)(2,1)} %bitcast.40), calls=%async_computation.1 | async-start | bytes 1048576 | tf_op jit(solution)/shard_map/all_to_all | solution.py:471
  168.0 1.7 copy-start.1
  211.1 1.0 copy-start.3
  212.1 0.7 copy-start.4
  212.8 0.7 copy-start.5
  213.5 0.7 copy-start.6
  214.1 0.7 copy-start.7
  225.5 0.8 copy-start.2
  285.5 15.7 %collective-permute-start.1 = (bf16[128,512]{1,0:T(8,128)(2,1)S(1)}, bf16[128,512]{1,0:T(8,128)(2,1)S(1)}, u32[]{:S(2)}, u32[]{:S(2)}) collective-permute-start(bf16[128,512]{1,0:T(8,128)(2,1)S(1)} %get-tuple-element.16), channel_id=1, source_target_pairs={{0,0},{1,8},{2,16},{3,24},{4,4},{5,12},{6,20},{7,28},{8,1},{9,9},{... | collective-permute-start | bytes 393224 | tf_op jit(solution)/shard_map/ppermute | solution.py:514
  289.3 14.1 %collective-permute-start.2 = (bf16[128,512]{1,0:T(8,128)(2,1)S(1)}, bf16[128,512]{1,0:T(8,128)(2,1)S(1)}, u32[]{:S(2)}, u32[]{:S(2)}) collective-permute-start(bf16[128,512]{1,0:T(8,128)(2,1)S(1)} %get-tuple-element.15), channel_id=1, source_target_pairs={{0,4},{1,12},{2,20},{3,28},{4,0},{5,8},{6,16},{7,24},{8,5},{9,13},... | collective-permute-start | bytes 393224 | tf_op jit(solution)/shard_map/ppermute | solution.py:514
Sparse Core Ops, SparseCore 0:
  8.9 16.7 all-gather.1
